TPU v7x, 256 devices: a whole 4x4x8 slice. The times are simulated.
256 devices in a mesh: ctx: 32 (over y, z), kvh: 8 (over x, core).
Axes of the slice: x: 4, y: 4, z: 8, core: 2. Of those that a mesh axis runs over, the one named last changes fastest.
Arguments:
- queries: bfloat16 [65536, 4096], P('ctx', 'kvh'), may hold values from -64 to 64
- keys: bfloat16 [65536, 1024], P('ctx', 'kvh'), may hold values from -4 to 4
- values: bfloat16 [65536, 1024], P('ctx', 'kvh'), may hold values from -6 to 6
- vertical: int32 [32, 512], P('kvh'), may hold values from 0 to 65535, as said below
Outputs:
- attended: bfloat16 [65536, 4096], P('ctx', 'kvh')
Inputs may be any that keep to these rules, and one draw needn't show every extreme that they name: `vertical`: each row holds 512 distinct positions in rising order; at most 32 of a row lie among the 2048 tokens of one device, and exactly 32 do for one device in every row.
All inputs are finite; a program needn't handle non-finite values.
Results may differ from a plain program's by a relative error of at most 0.0046.
Values may be sent and summed in bfloat16 or wider, within the bound.
No kernel may reach another device: no remote copies, remote signals or barrier semaphores. Data moves between devices by JAX's collectives and lax.ppermute only.
A program may use at most 64 MiB of HBM per device.

v0:
```python
import math

import jax
import jax.numpy as jnp
from jax import lax
from jax.sharding import PartitionSpec as P

BAND = 1024


def from_behind(array, axis, by):
    length = lax.axis_size(axis)
    pairs = [(i, i + by) for i in range(length) if 0 <= i + by < length]
    return lax.ppermute(array, axis, pairs)


def attend(qblk, band_kv, band_pos, vert_kv, vert_pos, qpos, width):
    head = qblk.shape[-1]
    scale = 1.0 / math.sqrt(head)
    band_s = (
        jnp.einsum("qhd,kd->hqk", qblk, band_kv[:, :head], preferred_element_type=jnp.float32)
        * scale
    )
    vert_s = (
        jnp.einsum("qhd,hcd->hqc", qblk, vert_kv[:, :, :head], preferred_element_type=jnp.float32)
        * scale
    )
    band_ok = (
        (band_pos[None, :] <= qpos[:, None])
        & (band_pos[None, :] > qpos[:, None] - width)
        & (band_pos[None, :] >= 0)
    )
    vert_ok = vert_pos[:, None, :] <= qpos[None, :, None] - width
    band_s = jnp.where(band_ok[None, :, :], band_s, -1e30)
    vert_s = jnp.where(vert_ok, vert_s, -1e30)
    scores = jnp.concatenate([vert_s, band_s], -1)
    top = jnp.max(scores, -1, keepdims=True)
    expo = jnp.exp(scores - top)
    total = jnp.sum(expo, -1)
    weight = expo.astype(jnp.bfloat16)
    ncols = vert_kv.shape[1]
    out = jnp.einsum(
        "hqc,hcd->qhd",
        weight[:, :, :ncols],
        vert_kv[:, :, head:],
        preferred_element_type=jnp.float32,
    )
    out = out + jnp.einsum(
        "hqk,kd->qhd", weight[:, :, ncols:], band_kv[:, head:], preferred_element_type=jnp.float32
    )
    out = out / jnp.transpose(total)[:, :, None]
    return out.astype(jnp.bfloat16).reshape(qblk.shape[0], -1)


def shards(queries, keys, values, vertical):
    tok = keys.shape[0]
    head = keys.shape[1]
    group = queries.shape[1] // head
    width = BAND
    block = min(512, tok)
    base = lax.axis_index("ctx") * tok
    paired = jnp.concatenate([keys, values], 1)
    edge = from_behind(paired[tok - width :], "ctx", 1)
    extended = jnp.concatenate([edge, paired], 0)
    local = vertical - base
    inside = (local >= 0) & (local < tok)
    rows = jnp.take(paired, jnp.clip(local, 0, tok - 1), axis=0)
    table = jnp.where(inside[:, :, None], rows, jnp.zeros_like(rows))
    vert_kv = lax.psum(table, "ctx").astype(jnp.float32).astype(jnp.bfloat16)
    queries3 = queries.reshape(tok, group, head)

    def one_block(start):
        qblk = lax.dynamic_slice_in_dim(queries3, start, block, 0)
        band_kv = lax.dynamic_slice_in_dim(extended, start, width + block, 0)
        band_pos = base + start - width + jnp.arange(width + block, dtype=jnp.int32)
        qpos = base + start + jnp.arange(block, dtype=jnp.int32)
        return attend(qblk, band_kv, band_pos, vert_kv, vertical, qpos, width)

    starts = jnp.arange(tok // block, dtype=jnp.int32) * block
    result = lax.map(one_block, starts)
    return result.reshape(tok, group * head)


def solution(mesh):
    in_specs = (P("ctx", "kvh"), P("ctx", "kvh"), P("ctx", "kvh"), P("kvh", None))
    out_specs = P("ctx", "kvh")
    return jax.shard_map(shards, mesh=mesh, in_specs=in_specs, out_specs=out_specs, check_vma=False)
```

profile of v0, /device:TPU:1, one launch (start us, length us, event | category | flops | bytes accessed | tf_op | source)
XLA Modules:
  0.0 272.7 jit_solution(703484851391934692)
XLA Ops:
  6.5 0.0 all-reduce.2.cloned.1.call-start
  6.5 0.7 fusion.28
  7.2 0.7 compare_and_fusion.1
  8.0 1.1 constant_dynamic-update-slice_fusion.2
  9.1 1.2 constant_dynamic-update-slice_fusion.1
  10.3 7.5 %gather_fusion = bf16[2048,256]{1,0:T(8,128)(2,1)S(1)} fusion(bf16[2048,256]{1,0:T(8,128)(2,1)S(1)} %constant_dynamic-update-slice_fusion.1, s32[2048]{0:T(1024)S(1)} %broadcast_clamp_fusion), kind=kCustom, calls=%fused_computation | custom fusion | bytes 2105344 | tf_op jit(solution)/shard_map/jit(_take)/gather | solution.py:67
  17.8 1.5 select_select_fusion
  19.3 0.0 all-reduce.2.cloned.1.call-update
  19.3 0.0 copy-start.1
  19.4 4.4 %collective-permute-start = (bf16[1024,256]{1,0:T(8,128)(2,1)S(1)}, bf16[1024,256]{1,0:T(8,128)(2,1)S(1)}, u32[]{:S(2)}, u32[]{:S(2)}) collective-permute-start(bf16[1024,256]{1,0:T(8,128)(2,1)S(1)} %slice.51), channel_id=1, source_target_pairs={{0,8},{8,16},{16,24},{24,32},{32,40},{40,48},{48,56},{56,64},{64,7... | collective-permute-start | bytes 1572872 | tf_op jit(solution)/shard_map/ppermute | solution.py:14
  23.8 4.0 %copy.14 = bf16[2048,512]{0,1:T(8,128)(2,1)} copy(bf16[2048,512]{1,0:T(8,128)(2,1)} %param.6) | data formatting | bytes 4194304 | tf_op args[0]
  27.8 6.7 %collective-permute-done = bf16[1024,256]{1,0:T(8,128)(2,1)S(1)} collective-permute-done((bf16[1024,256]{1,0:T(8,128)(2,1)S(1)}, bf16[1024,256]{1,0:T(8,128)(2,1)S(1)}, u32[]{:S(2)}, u32[]{:S(2)}) %collective-permute-start) | collective-permute-done | bytes 524320 | tf_op jit(solution)/shard_map/ppermute | solution.py:14
  34.5 1.3 pad_maximum_fusion
  35.8 132.4 %all-reduce.2.cloned.1.call-done = bf16[4,512,256]{2,1,0:T(8,128)(2,1)} async-done(((bf16[4,512,256]{2,1,0:T(8,128)(2,1)}), bf16[4,512,256]{2,1,0:T(8,128)(2,1)}) %all-reduce.2.cloned.1.call-update) | async-done | bytes 1048592 | tf_op jit(solution)/shard_map/psum | solution.py:69
  168.1 0.0 copy-done.1
  168.1 97.7 %while.13 = (s32[]{:T(128)}, bf16[4,512,512]{2,1,0:T(8,128)(2,1)}, s32[4,512]{1,0:T(4,128)S(1)}, s32[4]{0:T(128)S(1)}, s32[]{:T(128)}, /*index=5*/bf16[2048,4,12...) while((s32[]{:T(128)}, bf16[4,512,512]{2,1,0:T(8,128)(2,1)}, ...), condition=%wide.region_5.6_spmd, body=%wide.region_1.5_spmd.sunk | while | flops 2181826048 | bytes 65898284 | solution.py:80
  168.1 0.6 dynamic_slice.35
  169.3 1.1 and_and_fusion.2
  173.3 0.0 copy-start
  173.3 4.6 %fusion.42 = (f32[4,512]{1,0:T(4,128)S(1)}, f32[4,512,1536]{1,2,0:T(8,128)S(1)}) fusion(bf16[2048,4,128]{0,2,1:T(8,128)(2,1)} %get-tuple-element.262, s32[]{:T(128)S(6)} %select_n.57, bf16[3072,256]{1,0:T(8,128)(2,1)} %get-tuple-element.264, s32[]{:T(128)S(6)} %select_n.58, pred[512,1536]{0,1:T(8,128)(4,1)S(1)} %and_and_fusion.2), kind=kOutput, calls=%fused_computation.41.clone.1 | convolution fusion | flops 814741504 | bytes 14295048 | tf_op jit(solution)/shard_map/while/body/eval_jaxpr/qhd,kd->hqk/dot_general | solution.py:21
  177.9 0.0 copy-done
  177.9 2.1 fusion.43
  180.0 4.9 %fusion.44 = (f32[4,512]{1,0:T(4,128)S(1)}, bf16[4,512,2048]{1,2,0:T(8,128)(2,1)}) fusion(f32[4,512,1536]{1,2,0:T(8,128)S(1)} %get-tuple-element.223, f32[4,512,512]{1,2,0:T(8,128)S(1)} %get-tuple-element.224, f32[4,512]{1,0:T(4,128)S(1)} %reduce_max.31), kind=kLoop, calls=%fused_computation.4.clone.1 | loop fusion | flops 16775168 | bytes 25182208 | tf_op jit(solution)/shard_map/while/body/eval_jaxpr/reduce_sum | solution.py:39
  184.9 4.0 %fusion.45 = f32[512,4,128]{0,2,1:T(8,128)S(1)} fusion(bf16[4,512,2048]{1,2,0:T(8,128)(2,1)} %get-tuple-element.227, bf16[3072,256]{1,0:T(8,128)(2,1)} %get-tuple-element.264, s32[]{:T(128)S(6)} %select_n.58, s32[]{:T(128)S(6)} %add.162), kind=kOutput, calls=%fused_computation.13.clone.1 | convolution fusion | flops 805306368 | bytes 7733256 | tf_op jit(solution)/shard_map/while/body/eval_jaxpr/hqk,kd->qhd/dot_general | solution.py:48
  188.9 0.5 copy.27
  189.5 2.1 fusion.46
  191.5 0.2 copy.28
  191.8 0.8 constant_dynamic-update-slice_fusion.4
  192.6 0.6 dynamic_slice.35
  193.8 1.1 and_and_fusion.2
  197.7 0.0 copy-start
  197.7 4.6 %fusion.42 = (f32[4,512]{1,0:T(4,128)S(1)}, f32[4,512,1536]{1,2,0:T(8,128)S(1)}) fusion(bf16[2048,4,128]{0,2,1:T(8,128)(2,1)} %get-tuple-element.262, s32[]{:T(128)S(6)} %select_n.57, bf16[3072,256]{1,0:T(8,128)(2,1)} %get-tuple-element.264, s32[]{:T(128)S(6)} %select_n.58, pred[512,1536]{0,1:T(8,128)(4,1)S(1)} %and_and_fusion.2), kind=kOutput, calls=%fused_computation.41.clone.1 | convolution fusion | flops 814741504 | bytes 14295048 | tf_op jit(solution)/shard_map/while/body/eval_jaxpr/qhd,kd->hqk/dot_general | solution.py:21
  202.3 0.0 copy-done
  202.3 2.1 fusion.43
  204.4 4.9 %fusion.44 = (f32[4,512]{1,0:T(4,128)S(1)}, bf16[4,512,2048]{1,2,0:T(8,128)(2,1)}) fusion(f32[4,512,1536]{1,2,0:T(8,128)S(1)} %get-tuple-element.223, f32[4,512,512]{1,2,0:T(8,128)S(1)} %get-tuple-element.224, f32[4,512]{1,0:T(4,128)S(1)} %reduce_max.31), kind=kLoop, calls=%fused_computation.4.clone.1 | loop fusion | flops 16775168 | bytes 25182208 | tf_op jit(solution)/shard_map/while/body/eval_jaxpr/reduce_sum | solution.py:39
  209.3 4.0 %fusion.45 = f32[512,4,128]{0,2,1:T(8,128)S(1)} fusion(bf16[4,512,2048]{1,2,0:T(8,128)(2,1)} %get-tuple-element.227, bf16[3072,256]{1,0:T(8,128)(2,1)} %get-tuple-element.264, s32[]{:T(128)S(6)} %select_n.58, s32[]{:T(128)S(6)} %add.162), kind=kOutput, calls=%fused_computation.13.clone.1 | convolution fusion | flops 805306368 | bytes 7733256 | tf_op jit(solution)/shard_map/while/body/eval_jaxpr/hqk,kd->qhd/dot_general | solution.py:48
  213.4 0.5 copy.27
  213.9 2.1 fusion.46
  216.0 0.2 copy.28
  216.2 0.8 constant_dynamic-update-slice_fusion.4
  217.0 0.6 dynamic_slice.35
  218.2 1.1 and_and_fusion.2
  222.1 0.0 copy-start
  222.2 4.6 %fusion.42 = (f32[4,512]{1,0:T(4,128)S(1)}, f32[4,512,1536]{1,2,0:T(8,128)S(1)}) fusion(bf16[2048,4,128]{0,2,1:T(8,128)(2,1)} %get-tuple-element.262, s32[]{:T(128)S(6)} %select_n.57, bf16[3072,256]{1,0:T(8,128)(2,1)} %get-tuple-element.264, s32[]{:T(128)S(6)} %select_n.58, pred[512,1536]{0,1:T(8,128)(4,1)S(1)} %and_and_fusion.2), kind=kOutput, calls=%fused_computation.41.clone.1 | convolution fusion | flops 814741504 | bytes 14295048 | tf_op jit(solution)/shard_map/while/body/eval_jaxpr/qhd,kd->hqk/dot_general | solution.py:21
  226.7 0.0 copy-done
  226.8 2.1 fusion.43
  228.9 4.9 %fusion.44 = (f32[4,512]{1,0:T(4,128)S(1)}, bf16[4,512,2048]{1,2,0:T(8,128)(2,1)}) fusion(f32[4,512,1536]{1,2,0:T(8,128)S(1)} %get-tuple-element.223, f32[4,512,512]{1,2,0:T(8,128)S(1)} %get-tuple-element.224, f32[4,512]{1,0:T(4,128)S(1)} %reduce_max.31), kind=kLoop, calls=%fused_computation.4.clone.1 | loop fusion | flops 16775168 | bytes 25182208 | tf_op jit(solution)/shard_map/while/body/eval_jaxpr/reduce_sum | solution.py:39
  233.8 4.0 %fusion.45 = f32[512,4,128]{0,2,1:T(8,128)S(1)} fusion(bf16[4,512,2048]{1,2,0:T(8,128)(2,1)} %get-tuple-element.227, bf16[3072,256]{1,0:T(8,128)(2,1)} %get-tuple-element.264, s32[]{:T(128)S(6)} %select_n.58, s32[]{:T(128)S(6)} %add.162), kind=kOutput, calls=%fused_computation.13.clone.1 | convolution fusion | flops 805306368 | bytes 7733256 | tf_op jit(solution)/shard_map/while/body/eval_jaxpr/hqk,kd->qhd/dot_general | solution.py:48
  237.8 0.5 copy.27
  238.3 2.1 fusion.46
  240.4 0.2 copy.28
  240.6 0.8 constant_dynamic-update-slice_fusion.4
  241.5 0.6 dynamic_slice.35
  242.6 1.1 and_and_fusion.2
  246.6 0.0 copy-start
  246.6 4.6 %fusion.42 = (f32[4,512]{1,0:T(4,128)S(1)}, f32[4,512,1536]{1,2,0:T(8,128)S(1)}) fusion(bf16[2048,4,128]{0,2,1:T(8,128)(2,1)} %get-tuple-element.262, s32[]{:T(128)S(6)} %select_n.57, bf16[3072,256]{1,0:T(8,128)(2,1)} %get-tuple-element.264, s32[]{:T(128)S(6)} %select_n.58, pred[512,1536]{0,1:T(8,128)(4,1)S(1)} %and_and_fusion.2), kind=kOutput, calls=%fused_computation.41.clone.1 | convolution fusion | flops 814741504 | bytes 14295048 | tf_op jit(solution)/shard_map/while/body/eval_jaxpr/qhd,kd->hqk/dot_general | solution.py:21
  251.2 0.0 copy-done
  251.2 2.1 fusion.43
  253.3 4.9 %fusion.44 = (f32[4,512]{1,0:T(4,128)S(1)}, bf16[4,512,2048]{1,2,0:T(8,128)(2,1)}) fusion(f32[4,512,1536]{1,2,0:T(8,128)S(1)} %get-tuple-element.223, f32[4,512,512]{1,2,0:T(8,128)S(1)} %get-tuple-element.224, f32[4,512]{1,0:T(4,128)S(1)} %reduce_max.31), kind=kLoop, calls=%fused_computation.4.clone.1 | loop fusion | flops 16775168 | bytes 25182208 | tf_op jit(solution)/shard_map/while/body/eval_jaxpr/reduce_sum | solution.py:39
  258.2 4.0 %fusion.45 = f32[512,4,128]{0,2,1:T(8,128)S(1)} fusion(bf16[4,512,2048]{1,2,0:T(8,128)(2,1)} %get-tuple-element.227, bf16[3072,256]{1,0:T(8,128)(2,1)} %get-tuple-element.264, s32[]{:T(128)S(6)} %select_n.58, s32[]{:T(128)S(6)} %add.162), kind=kOutput, calls=%fused_computation.13.clone.1 | convolution fusion | flops 805306368 | bytes 7733256 | tf_op jit(solution)/shard_map/while/body/eval_jaxpr/hqk,kd->qhd/dot_general | solution.py:48
  262.2 0.5 copy.27
  262.7 2.1 fusion.46
  264.8 0.2 copy.28
  265.0 0.8 constant_dynamic-update-slice_fusion.4
  (21 shorter events, 0.2 us)
Async XLA Ops:
  6.5 161.6 %all-reduce.2.cloned.1.call-start = ((), (), s32[]{:S(2)}) async-start(), calls=%async_computation | async-start | bytes 2097152 | tf_op jit(solution)/shard_map/psum | solution.py:69
  19.3 148.8 %copy-start.1 = (s32[4,512]{1,0:T(4,128)S(1)}, s32[4,512]{1,0:T(4,128)}, u32[]{:S(2)}) copy-start(s32[4,512]{1,0:T(4,128)} %param.9) | copy-start | bytes 24580
  19.4 15.1 %collective-permute-start = (bf16[1024,256]{1,0:T(8,128)(2,1)S(1)}, bf16[1024,256]{1,0:T(8,128)(2,1)S(1)}, u32[]{:S(2)}, u32[]{:S(2)}) collective-permute-start(bf16[1024,256]{1,0:T(8,128)(2,1)S(1)} %slice.51), channel_id=1, source_target_pairs={{0,8},{8,16},{16,24},{24,32},{32,40},{40,48},{48,56},{56,64},{64,7... | collective-permute-start | bytes 1572872 | tf_op jit(solution)/shard_map/ppermute | solution.py:14
  173.3 4.6 %copy-start = (bf16[4,512,256]{2,1,0:T(8,128)(2,1)S(1)}, bf16[4,512,256]{2,1,0:T(8,128)(2,1)}, u32[]{:S(2)}) copy-start(bf16[4,512,256]{2,1,0:T(8,128)(2,1)} %get-tuple-element.263) | copy-start | bytes 3145732 | tf_op jit(solution)/shard_map/while
  197.7 4.6 %copy-start = (bf16[4,512,256]{2,1,0:T(8,128)(2,1)S(1)}, bf16[4,512,256]{2,1,0:T(8,128)(2,1)}, u32[]{:S(2)}) copy-start(bf16[4,512,256]{2,1,0:T(8,128)(2,1)} %get-tuple-element.263) | copy-start | bytes 3145732 | tf_op jit(solution)/shard_map/while
  222.1 4.6 %copy-start = (bf16[4,512,256]{2,1,0:T(8,128)(2,1)S(1)}, bf16[4,512,256]{2,1,0:T(8,128)(2,1)}, u32[]{:S(2)}) copy-start(bf16[4,512,256]{2,1,0:T(8,128)(2,1)} %get-tuple-element.263) | copy-start | bytes 3145732 | tf_op jit(solution)/shard_map/while
  246.6 4.6 %copy-start = (bf16[4,512,256]{2,1,0:T(8,128)(2,1)S(1)}, bf16[4,512,256]{2,1,0:T(8,128)(2,1)}, u32[]{:S(2)}) copy-start(bf16[4,512,256]{2,1,0:T(8,128)(2,1)} %get-tuple-element.263) | copy-start | bytes 3145732 | tf_op jit(solution)/shard_map/while
Sparse Core Ops, SparseCore 0:
  19.4 148.6 all-reduce.1
where the time goes:
time: 277 us; the launch traced here: 273 us
  waiting for transfers between devices  139 us (50%)
  matrix products  51 us (18%)
  other arithmetic  28.5 us (10%)
  local copies, waits for them, and re-layouts  22.5 us (8%)
  loops' own time  13.8 us (5%)
  between operations  13.5 us (5%)
  starting transfers between devices  4.41 us (2%)
    psum x1, waiting for transfers between devices, shards(): vert_kv = lax.psum(table, 'ctx').astype(jnp.float32).astype(jnp.bfloat16)  132 us
    reduce_sum x4, other arithmetic, attend(): total = jnp.sum(expo, -1)  19.6 us
    dot_general x4, matrix products, attend(): jnp.einsum('qhd,kd->hqk', qblk, band_kv[:, :head], preferred_element_type...  18.3 us
    dot_general x4, matrix products, attend(): jnp.einsum('hqk,kd->qhd', weight[:, :, ncols:], band_kv[:, head:], prefer...  16.1 us
    another operation x1, loops' own time, shards(): result = lax.map(one_block, starts)  13.8 us
    dot_general x4, matrix products, attend(): jnp.einsum('qhd,hcd->hqc', qblk, vert_kv[:, :, :head], preferred_element_...  8.33 us
    dot_general x4, matrix products, attend(): jnp.einsum('hqc,hcd->qhd', weight[:, :, :ncols], vert_kv[:, :, head:], pr...  8.25 us
    gather x1, local copies, waits for them, and re-layouts, shards(): rows = jnp.take(paired, jnp.clip(local, 0, tok - 1), axis=0)  7.5 us
  transfers between devices with their start and end apart: 2, of which 2 were waited for; matrix products, arithmetic and copies ran while one was open for 2% of the time, Pallas kernels for 0%

commit v1 on v0

v1 whole, which is shorter than its diff:
```python
import math
import jax
import jax.numpy as jnp
from jax import lax
from jax.experimental import pallas as pl
from jax.experimental.pallas import tpu as pltpu
from jax.sharding import PartitionSpec as P
TOK=2048; HEAD=128; GROUP=4; COLS=512; BAND=1024; CAP=32; NCTX=32
QB=256
C=math.log2(math.e)/math.sqrt(HEAD)
F32=jnp.float32; BF=jnp.bfloat16
NEG=-1e30

def dot(a,b): return jnp.dot(a,b,preferred_element_type=F32)

def pick_kernel(base_ref, vert_ref, k_ref, v_ref, out_ref):
    base=base_ref[0]
    vert=vert_ref[...]
    cols=lax.broadcasted_iota(jnp.int32,(CAP,COLS),1)
    slot=lax.broadcasted_iota(jnp.int32,(CAP,COLS),0)
    toks=lax.broadcasted_iota(jnp.int32,(CAP,TOK),1)
    rows=[]
    for h in range(GROUP):
        v=vert[h:h+1,:]-base
        start=jnp.sum((v<0).astype(jnp.int32),axis=1,keepdims=True)
        hit=(cols-start==slot)&(v<TOK)
        pos=jnp.sum(jnp.where(hit,v+1,0),axis=1,keepdims=True)-1
        rows.append((toks==pos).astype(F32).astype(BF))
    sel=jnp.concatenate(rows,0)
    out_ref[:,:HEAD]=dot(sel,k_ref[...]).astype(BF)
    out_ref[:,HEAD:]=dot(sel,v_ref[...]).astype(BF)

def pick(base,vertical,keys,values):
    return pl.pallas_call(pick_kernel,
        out_shape=jax.ShapeDtypeStruct((GROUP*CAP,2*HEAD),BF),
        in_specs=[pl.BlockSpec(memory_space=pltpu.SMEM)]+[pl.BlockSpec(memory_space=pltpu.VMEM)]*3,
        out_specs=pl.BlockSpec(memory_space=pltpu.VMEM),
        compiler_params=pltpu.CompilerParams(vmem_limit_bytes=16<<20),
        name="pick")(base,vertical,keys,values)

def band_kernel(first_ref, q_ref, k0_ref, k1_ref, v0_ref, v1_ref, acc_ref, ml_ref, kt, vx):
    step=pl.program_id(0)
    @pl.when(step==0)
    def _():
        first=first_ref[0]!=0
        k0=jnp.where(first,jnp.broadcast_to(k1_ref[0:1,:],k0_ref.shape),k0_ref[...])
        kt[:,:BAND]=k0.T
        kt[:,BAND:]=k1_ref[...].T
        one=jnp.ones((BAND,HEAD),BF)
        zero=jnp.zeros((BAND,HEAD),BF)
        vx[:BAND,:HEAD]=jnp.where(first,zero,v0_ref[...])
        vx[:BAND,HEAD:]=jnp.where(first,zero,one)
        vx[BAND:,:HEAD]=v1_ref[...]
        vx[BAND:,HEAD:]=one
    off=pl.multiple_of(step*QB,QB)
    tri=lax.broadcasted_iota(jnp.int32,(QB,QB),1)<=lax.broadcasted_iota(jnp.int32,(QB,QB),0)
    lane=lax.broadcasted_iota(jnp.int32,(QB,HEAD),1)
    ml=jnp.zeros((QB,HEAD),F32)
    for h in range(GROUP):
        q=q_ref[:,h*HEAD:(h+1)*HEAD]
        s=dot(q,kt[:,pl.ds(off,BAND+QB)])
        s_in=s[:,QB:BAND]
        s_edge=jnp.where(tri,s[:,BAND:],s[:,:QB])
        m=jnp.maximum(jnp.max(s_in,axis=1,keepdims=True),jnp.max(s_edge,axis=1,keepdims=True))
        p_in=jnp.exp2((s_in-m)*C).astype(BF)
        p_edge=jnp.exp2((s_edge-m)*C)
        p_last=jnp.where(tri,p_edge,0.0).astype(BF)
        p_first=jnp.where(tri,0.0,p_edge).astype(BF)
        p=jnp.concatenate([p_first,p_in,p_last],1)
        o=dot(p,vx[pl.ds(off,BAND+QB),:])
        acc_ref[:,h*HEAD:(h+1)*HEAD]=o[:,:HEAD]
        ml=jnp.where(lane==h,m,jnp.where(lane==GROUP+h,o[:,HEAD:],ml))
    ml_ref[...]=ml

def band(first,queries,qhalf,k0,k1,v0,v1,bk0,bk1):
    n=BAND//QB
    kspec=lambda b: pl.BlockSpec((BAND,HEAD),lambda i: (b,0))
    return pl.pallas_call(band_kernel,
        grid=(n,),
        out_shape=(jax.ShapeDtypeStruct((BAND,GROUP*HEAD),F32),jax.ShapeDtypeStruct((BAND,HEAD),F32)),
        in_specs=[pl.BlockSpec(memory_space=pltpu.SMEM),
            pl.BlockSpec((QB,GROUP*HEAD),lambda i:(qhalf*n+i,0)),kspec(bk0),kspec(bk1),kspec(bk0),kspec(bk1)],
        out_specs=(pl.BlockSpec((QB,GROUP*HEAD),lambda i:(i,0)),pl.BlockSpec((QB,HEAD),lambda i:(i,0))),
        scratch_shapes=[pltpu.VMEM((HEAD,2*BAND),BF),pltpu.VMEM((2*BAND,2*HEAD),BF)],
        compiler_params=pltpu.CompilerParams(vmem_limit_bytes=32<<20),
        cost_estimate=pl.CostEstimate(flops=4*BAND*GROUP*HEAD*(BAND+QB),bytes_accessed=6<<20,transcendentals=BAND*BAND*GROUP),
        name="band")(first,queries,k0,k1,v0,v1)

def vert_kernel(base_ref, q_ref, g_ref, vert_ref, vertt_ref, code_ref, a0_ref, ml0_ref, a1_ref, ml1_ref, out_ref, kt, vx):
    step=pl.program_id(0)
    @pl.when(step==0)
    def _():
        lanes=lax.broadcasted_iota(jnp.int32,(COLS,HEAD),1)
        rows=lax.broadcasted_iota(jnp.int32,(COLS,1),0)
        code=code_ref[...]
        for h in range(GROUP):
            v=vertt_ref[:,h:h+1]
            starts=jnp.sum((v<lanes*TOK).astype(jnp.int32),axis=0,keepdims=True)
            d=v//TOK
            start=jnp.sum(jnp.where(lanes==d,starts,0),axis=1,keepdims=True)
            mine=d*CAP+rows-start
            sel=(mine==code).astype(F32).astype(BF)
            t=dot(sel,g_ref[:,h*CAP:(h+1)*CAP,:].reshape(NCTX*CAP,2*HEAD))
            kt[h]=t[:,:HEAD].astype(BF).T
            vx[h,:,:HEAD]=t[:,HEAD:].astype(BF)
            vx[h,:,HEAD:]=jnp.ones((COLS,HEAD),BF)
    half=(TOK//QB)//2
    def body(a_ref,ml_ref):
        qpos=base_ref[0]+step*QB-BAND+lax.broadcasted_iota(jnp.int32,(QB,1),0)
        ml=ml_ref[...]
        for h in range(GROUP):
            s=dot(q_ref[:,h*HEAD:(h+1)*HEAD],kt[h])
            s=jnp.where(vert_ref[h:h+1,:]<=qpos,s,NEG)
            mb=ml[:,h:h+1]; lb=ml[:,GROUP+h:GROUP+h+1]
            m=jnp.maximum(jnp.max(s,axis=1,keepdims=True),mb)
            p=jnp.exp2((s-m)*C).astype(BF)
            o=dot(p,vx[h])
            alpha=jnp.exp2((mb-m)*C)
            num=a_ref[:,h*HEAD:(h+1)*HEAD]*alpha+o[:,:HEAD]
            den=o[:,HEAD:]+lb*alpha
            out_ref[:,h*HEAD:(h+1)*HEAD]=(num/den).astype(BF)
    @pl.when(step<half)
    def _(): body(a0_ref,ml0_ref)
    @pl.when(step>=half)
    def _(): body(a1_ref,ml1_ref)

def vert(base,queries,gathered,vertical,vertt,code,a0,ml0,a1,ml1):
    n=TOK//QB
    full=lambda *s: pl.BlockSpec(s,lambda i:(0,)*len(s))
    lo=lambda i:(jnp.minimum(i,n//2-1),0)
    hi=lambda i:(jnp.maximum(i-n//2,0),0)
    return pl.pallas_call(vert_kernel,
        grid=(n,),
        out_shape=jax.ShapeDtypeStruct((TOK,GROUP*HEAD),BF),
        in_specs=[pl.BlockSpec(memory_space=pltpu.SMEM),
            pl.BlockSpec((QB,GROUP*HEAD),lambda i:(i,0)),
            full(NCTX,GROUP*CAP,2*HEAD),full(GROUP,COLS),full(COLS,GROUP),full(1,NCTX*CAP),
            pl.BlockSpec((QB,GROUP*HEAD),lo),pl.BlockSpec((QB,HEAD),lo),
            pl.BlockSpec((QB,GROUP*HEAD),hi),pl.BlockSpec((QB,HEAD),hi)],
        out_specs=pl.BlockSpec((QB,GROUP*HEAD),lambda i:(i,0)),
        scratch_shapes=[pltpu.VMEM((GROUP,HEAD,COLS),BF),pltpu.VMEM((GROUP,COLS,2*HEAD),BF)],
        compiler_params=pltpu.CompilerParams(vmem_limit_bytes=40<<20),
        cost_estimate=pl.CostEstimate(flops=4*TOK*GROUP*HEAD*COLS,bytes_accessed=12<<20,transcendentals=TOK*COLS*GROUP),
        name="vert")(base,queries,gathered,vertical,vertt,code,a0,ml0,a1,ml1)


AXES = ("ctx", "kvh")


def hop(array, grid, step):
    ny, nz = grid
    nk = lax.axis_size("kvh")
    pairs = []
    for y in range(ny):
        for z in range(nz):
            for k in range(nk):
                s = 1 if k % 2 == 0 else -1
                to = ((y + s * step[0]) % ny) * nz + (z + s * step[1]) % nz
                pairs.append(((y * nz + z) * nk + k, to * nk + k))
    return lax.ppermute(array, AXES, pairs)


def widen(array, came, grid, steps):
    parts = [array] + [hop(array, grid, s) for s in steps]
    origin = list(came)
    for s in steps:
        origin += [(o[0] - s[0], o[1] - s[1]) for o in came]
    return jnp.concatenate(parts, 0), origin


def spread(own):
    grid = (4, 8)
    held, came = widen(own[None], [(0, 0)], grid, ((0, 2), (0, 4), (0, -2)))
    held, came = widen(held, came, grid, ((2, 0), (1, 1), (-1, 1)))
    even = held[:8]
    a = hop(even, grid, (1, 0))
    b = hop(even, grid, (0, 1))
    came = came + [(y - 1, z) for y, z in came[:8]] + [(y, z - 1) for y, z in came[:8]]
    return jnp.concatenate([held, a, b], 0), came


def shards(queries, keys, values, vertical):
    ctx = lax.axis_index("ctx")
    base = (ctx * TOK).astype(jnp.int32)[None]
    inner = jnp.zeros((1,), jnp.int32)
    first = (ctx == 0).astype(jnp.int32)[None]

    own = pick(base, vertical, keys, values)
    shift = [(i, i + 1) for i in range(NCTX - 1)]
    edge_k = lax.ppermute(keys[TOK - BAND :], "ctx", shift)
    edge_v = lax.ppermute(values[TOK - BAND :], "ctx", shift)
    gathered, came = spread(own)

    sign = 1 - 2 * (lax.axis_index("kvh") % 2)
    oy = jnp.asarray([o[0] for o in came], jnp.int32)
    oz = jnp.asarray([o[1] for o in came], jnp.int32)
    device = ((ctx // 8 + sign * oy) % 4) * 8 + (ctx % 8 + sign * oz) % 8
    code = (device[:, None] * CAP + jnp.arange(CAP, dtype=jnp.int32)[None, :]).reshape(1, -1)

    acc1, ml1 = band(inner, queries, 1, keys, keys, values, values, 0, 1)
    acc0, ml0 = band(first, queries, 0, edge_k, keys, edge_v, values, 0, 0)
    return vert(base, queries, gathered, vertical, vertical.T, code, acc0, ml0, acc1, ml1)


def solution(mesh):
    in_specs = (P("ctx", "kvh"), P("ctx", "kvh"), P("ctx", "kvh"), P("kvh", None))
    return jax.shard_map(shards, mesh=mesh, in_specs=in_specs, out_specs=P("ctx", "kvh"), check_vma=False)
```

time: 277 us -> 91.2 us (0.33); the launches traced: 273 us -> 90.7 us
  waiting for transfers between devices: 139 us -> 6.27 us
  matrix products: 51 us -> 0 us
  Pallas kernels: 0 us -> 40.4 us
  other arithmetic: 28.5 us -> 1.75 us
  starting transfers between devices: 4.41 us -> 26.7 us
  loops' own time: 13.8 us -> 0 us
  between operations: 13.5 us -> 0.19 us
  local copies, waits for them, and re-layouts: 22.5 us -> 15.3 us
    psum x1 -> x0, waiting for transfers between devices: 132 us -> none  [shards(): vert_kv = lax.psum(table, 'ctx').astype(jnp.float32).astype(jnp.bfloat16)]
    dot_general x16 -> x0, matrix products: 51 us -> none  [the longest x4 18.3 us: attend(): jnp.einsum('qhd,kd->hqk', qblk, band_kv[:, :head], preferred_element_type...]
    pallas_call x0 -> x4, Pallas kernels: none -> 40.4 us  [the longest x1 20 us: vert(): pl.pallas_call(vert_kernel, grid=(n,), out_shape=jax.ShapeDtypeStruct((TO...]
    ppermute x1 -> x10, starting transfers between devices: 4.4 us -> 26.7 us  [the longest x8 21.4 us: hop(): return lax.ppermute(array, AXES, pairs)]
    reduce_sum x4 -> x0, other arithmetic: 19.6 us -> none  [attend(): total = jnp.sum(expo, -1)]
    another operation x1 -> x0, loops' own time: 13.8 us -> none  [shards(): result = lax.map(one_block, starts)]
    unnamed x5 -> x38, local copies, waits for them, and re-layouts: 5.11 us -> 13 us
    gather x1 -> x0, local copies, waits for them, and re-layouts: 7.5 us -> none  [shards(): rows = jnp.take(paired, jnp.clip(local, 0, tok - 1), axis=0)]
  transfers between devices with their start and end apart: 2 -> 10, of which waited for: 2 -> 1; matrix products, arithmetic and copies ran while one was open for 2% -> 11% of each run, Pallas kernels for 0% -> 22%
where the time goes in v1:
time: 91.2 us; the launch traced here: 90.7 us
  Pallas kernels  40.4 us (44%)
  starting transfers between devices  26.7 us (29%)
  local copies, waits for them, and re-layouts  15.3 us (17%)
  waiting for transfers between devices  6.27 us (7%)
  other arithmetic  1.75 us (2%)
    ppermute x8, starting transfers between devices, hop(): return lax.ppermute(array, AXES, pairs)  21.4 us
    pallas_call x1, Pallas kernels, vert(): pl.pallas_call(vert_kernel, grid=(n,), out_shape=jax.ShapeDtypeStruct((TO...  20 us
    pallas_call x2, Pallas kernels, band(): pl.pallas_call(band_kernel, grid=(n,), out_shape=(jax.ShapeDtypeStruct((B...  19.7 us
    unnamed x38, local copies, waits for them, and re-layouts  13 us
    ppermute x8, waiting for transfers between devices, hop(): return lax.ppermute(array, AXES, pairs)  6.26 us
    ppermute x1, starting transfers between devices, shards(): edge_v = lax.ppermute(values[TOK - BAND:], 'ctx', shift)  3.36 us
    ppermute x1, starting transfers between devices, shards(): edge_k = lax.ppermute(keys[TOK - BAND:], 'ctx', shift)  1.99 us
  transfers between devices with their start and end apart: 10, of which 1 were waited for; matrix products, arithmetic and copies ran while one was open for 11% of the time, Pallas kernels for 22%

profile of v1, /device:TPU:1, one launch (start us, length us, event | category | flops | bytes accessed | tf_op | source)
XLA Modules:
  0.0 90.7 jit_solution(17737478011945716233)
XLA Ops:
  0.0 0.0 copy-start.5
  0.0 1.0 %copy-done.5 = bf16[2048,128]{1,0:T(8,128)(2,1)S(1)} copy-done((bf16[2048,128]{1,0:T(8,128)(2,1)S(1)}, bf16[2048,128]{1,0:T(8,128)(2,1)}, u32[]{:S(2)}) %copy-start.5) | copy-done | bytes 524312
  1.0 0.0 copy-start.7
  1.0 1.0 %copy-done.7 = bf16[2048,128]{1,0:T(8,128)(2,1)S(1)} copy-done((bf16[2048,128]{1,0:T(8,128)(2,1)S(1)}, bf16[2048,128]{1,0:T(8,128)(2,1)}, u32[]{:S(2)}) %copy-start.7) | copy-done | bytes 524312
  2.1 0.0 copy-start.11
  2.1 0.7 copy-done.11
  2.8 0.0 copy-start.6
  2.8 0.0 copy-start.8
  2.8 0.7 pick.1
  3.5 3.9 %collective-permute-start.2 = (bf16[1,128,256]{2,1,0:T(8,128)(2,1)S(1)}, bf16[1,128,256]{2,1,0:T(8,128)(2,1)S(1)}, u32[]{:S(2)}, u32[]{:S(2)}) collective-permute-start(bf16[1,128,256]{2,1,0:T(8,128)(2,1)S(1)} %bitcast.7), channel_id=1, source_target_pairs={{0,48},{1,17},{2,50},{3,19},{4,52},{5,21},{6,54},{7,23},{8,56},{9,... | collective-permute-start | bytes 196616 | tf_op jit(solution)/shard_map/ppermute | solution.py:160
  7.4 5.1 %collective-permute-start.1 = (bf16[1,128,256]{2,1,0:T(8,128)(2,1)S(1)}, bf16[1,128,256]{2,1,0:T(8,128)(2,1)S(1)}, u32[]{:S(2)}, u32[]{:S(2)}) collective-permute-start(bf16[1,128,256]{2,1,0:T(8,128)(2,1)S(1)} %bitcast.8), channel_id=1, source_target_pairs={{0,32},{1,33},{2,34},{3,35},{4,36},{5,37},{6,38},{7,39},{8,40},{9,... | collective-permute-start | bytes 196616 | tf_op jit(solution)/shard_map/ppermute | solution.py:160
  12.5 2.4 %collective-permute-start = (bf16[1,128,256]{2,1,0:T(8,128)(2,1)S(1)}, bf16[1,128,256]{2,1,0:T(8,128)(2,1)}, u32[]{:S(2)}, u32[]{:S(2)}) collective-permute-start(bf16[1,128,256]{2,1,0:T(8,128)(2,1)S(1)} %bitcast.9), channel_id=1, source_target_pairs={{0,16},{1,49},{2,18},{3,51},{4,20},{5,53},{6,22},{7,55},{8,24},{9,... | collective-permute-start | bytes 196616 | tf_op jit(solution)/shard_map/ppermute | solution.py:160
  14.9 0.7 slice.9
  15.6 3.4 %collective-permute-start.9 = (bf16[1024,128]{1,0:T(8,128)(2,1)}, bf16[1024,128]{1,0:T(8,128)(2,1)}, u32[]{:S(2)}, u32[]{:S(2)}) collective-permute-start(bf16[1024,128]{1,0:T(8,128)(2,1)} %slice.9), channel_id=1, source_target_pairs={{0,8},{8,16},{16,24},{24,32},{32,40},{40,48},{48,56},{56,64},{64,7... | collective-permute-start | bytes 786440 | tf_op jit(solution)/shard_map/ppermute | solution.py:191
  19.0 0.7 slice.8
  19.7 2.0 %collective-permute-start.8 = (bf16[1024,128]{1,0:T(8,128)(2,1)}, bf16[1024,128]{1,0:T(8,128)(2,1)}, u32[]{:S(2)}, u32[]{:S(2)}) collective-permute-start(bf16[1024,128]{1,0:T(8,128)(2,1)} %slice.8), channel_id=1, source_target_pairs={{0,8},{8,16},{16,24},{24,32},{32,40},{40,48},{48,56},{56,64},{64,7... | collective-permute-start | bytes 786440 | tf_op jit(solution)/shard_map/ppermute | solution.py:190
  21.7 0.6 constant_dynamic-update-slice_fusion.4
  22.3 0.0 copy-done.6
  22.3 0.0 copy-done.8
  22.3 0.0 copy-start
  22.3 1.6 %copy-done = bf16[2048,512]{1,0:T(8,128)(2,1)S(1)} copy-done((bf16[2048,512]{1,0:T(8,128)(2,1)S(1)}, bf16[2048,512]{1,0:T(8,128)(2,1)}, u32[]{:S(2)}) %copy-start) | copy-done | bytes 2097176
  23.9 0.0 copy-start.13
  23.9 0.0 copy-start.14
  23.9 0.0 copy-start.12
  23.9 9.2 %band.3 = (f32[1024,512]{1,0:T(8,128)S(1)}, f32[1024,128]{1,0:T(8,128)S(1)}) custom-call(s32[1]{0:T(128)} %constant.74.clone.1.first_ref, bf16[2048,512]{1,0:T(8,128)(2,1)S(1)} %copy-done, bf16[2048,128]{1,0:T(8,128)(2,1)S(1)} %copy-done.6, bf16[2048,128]{1,0:T(8,128)(2,1)S(1)} %copy-done.6, bf16[2048,128]{1,0:T(8,128)(2,1)S(1)} %copy-done.8, ...), custom_call_target="tpu_custom_call" | custom-call | flops 2684354560 | bytes 6291456 | tf_op jit(solution)/shard_map/band/pallas_call | solution.py:78
  33.2 0.0 copy-start.3
  33.2 1.3 %copy-done.3 = f32[1024,512]{1,0:T(8,128)} copy-done((f32[1024,512]{1,0:T(8,128)}, f32[1024,512]{1,0:T(8,128)S(1)}, u32[]{:S(2)}) %copy-start.3) | copy-done | bytes 2097176
  34.5 0.0 copy-done.13
  34.5 0.0 copy-done.14
  34.5 0.0 collective-permute-done.2
  34.5 0.0 collective-permute-done.1
  34.5 0.0 collective-permute-done
  34.5 1.7 %pad_maximum_fusion = bf16[4,128,256]{2,1,0:T(8,128)(2,1)} fusion(bf16[1,128,256]{2,1,0:T(8,128)(2,1)S(1)} %collective-permute-done.2, bf16[1,128,256]{2,1,0:T(8,128)(2,1)S(1)} %collective-permute-done.1, bf16[1,128,256]{2,1,0:T(8,128)(2,1)} %collective-permute-done, bf16[1,128,256]{2,1,0:T(8,128)(2,1)S(1)} %bitcast.10), kind=kLoop, calls=%fused_computation | loop fusion | flops 393216 | bytes 524288 | tf_op jit(solution)/shard_map/concatenate | solution.py:168
  36.2 0.0 collective-permute-start.4
  36.2 5.7 %collective-permute-start.3 = (bf16[4,128,256]{2,1,0:T(8,128)(2,1)}, bf16[4,128,256]{2,1,0:T(8,128)(2,1)S(1)}, u32[]{:S(2)}, u32[]{:S(2)}) collective-permute-start(bf16[4,128,256]{2,1,0:T(8,128)(2,1)} %pad_maximum_fusion), channel_id=1, source_target_pairs={{0,128},{1,129},{2,130},{3,131},{4,132},{5,133},{6,134},{7,135},{8... | collective-permute-start | bytes 786440 | tf_op jit(solution)/shard_map/ppermute | solution.py:160
  41.9 1.5 %constant_dynamic-update-slice_fusion.3 = (bf16[8,128,256]{2,1,0:T(8,128)(2,1)}, bf16[32,128,256]{2,1,0:T(8,128)(2,1)S(1)}) fusion(bf16[8,128,256]{2,1,0:T(8,128)(2,1)} %get-tuple-element.21, bf16[1,128,256]{2,1,0:T(8,128)(2,1)} %collective-permute-done, bf16[32,128,256]{2,1,0:T(8,128)(2,1)S(1)} %get-tuple-element.22), kind=kLoop, calls=%fused_computation.4 | loop fusion | bytes 196608
  43.4 0.6 constant_dynamic-update-slice_fusion.2
  44.0 0.6 constant_dynamic-update-slice_fusion.1
  44.6 6.2 %collective-permute-done.3 = bf16[4,128,256]{2,1,0:T(8,128)(2,1)S(1)} collective-permute-done((bf16[4,128,256]{2,1,0:T(8,128)(2,1)}, bf16[4,128,256]{2,1,0:T(8,128)(2,1)S(1)}, u32[]{:S(2)}, u32[]{:S(2)}) %collective-permute-start.3) | collective-permute-done | bytes 262176 | tf_op jit(solution)/shard_map/ppermute | solution.py:160
  50.9 0.7 constant_dynamic-update-slice_fusion
  51.6 0.0 copy-done.9
  51.6 0.6 collective-permute-start.6
  52.2 0.1 iota_add_fusion
  52.3 0.0 copy-done.12
  52.3 0.1 copy.7
  52.4 0.1 add.68.code_ref
  52.5 2.2 %collective-permute-start.5 = (bf16[4,128,256]{2,1,0:T(8,128)(2,1)}, bf16[4,128,256]{2,1,0:T(8,128)(2,1)S(1)}, u32[]{:S(2)}, u32[]{:S(2)}) collective-permute-start(bf16[4,128,256]{2,1,0:T(8,128)(2,1)} %pad_maximum_fusion), channel_id=1, source_target_pairs={{0,200},{1,121},{2,202},{3,123},{4,204},{5,125},{6,206},{7,127},{8... | collective-permute-start | bytes 786440 | tf_op jit(solution)/shard_map/ppermute | solution.py:160
  54.7 0.0 collective-permute-done.9.v0_ref
  54.7 1.5 %collective-permute-start.7 = (bf16[8,128,256]{2,1,0:T(8,128)(2,1)}, bf16[8,128,256]{2,1,0:T(8,128)(2,1)S(1)}, u32[]{:S(2)}, u32[]{:S(2)}) collective-permute-start(bf16[8,128,256]{2,1,0:T(8,128)(2,1)} %get-tuple-element.13), channel_id=1, source_target_pairs={{0,8},{1,57},{2,10},{3,59},{4,12},{5,61},{6,14},{7,63},{8,16},{9,1... | collective-permute-start | bytes 1572872 | tf_op jit(solution)/shard_map/ppermute | solution.py:160
  56.2 0.0 collective-permute-done.8.k0_ref
  56.2 1.6 %copy-done.1 = bf16[2048,512]{1,0:T(8,128)(2,1)S(1)} copy-done((bf16[2048,512]{1,0:T(8,128)(2,1)S(1)}, bf16[2048,512]{1,0:T(8,128)(2,1)}, u32[]{:S(2)}) %copy-start.1) | copy-done | bytes 2097176
  57.8 10.5 %band.2 = (f32[1024,512]{1,0:T(8,128)S(1)}, f32[1024,128]{1,0:T(8,128)S(1)}) custom-call(s32[1]{0:T(128)} %bitcast.3.first_ref, bf16[2048,512]{1,0:T(8,128)(2,1)S(1)} %copy-done.1, bf16[1024,128]{1,0:T(8,128)(2,1)} %collective-permute-done.8.k0_ref, bf16[2048,128]{1,0:T(8,128)(2,1)S(1)} %copy-done.6, bf16[1024,128]{1,0:T(8,128)(2,1)} %collective-permute-done.9.v0_ref, ...), custom_call_target="tpu_custom_call" | custom-call | flops 2684354560 | bytes 6291456 | tf_op jit(solution)/shard_map/band/pallas_call | solution.py:78
  68.3 0.0 copy-start.2
  68.3 0.0 copy-start.10
  68.3 0.0 collective-permute-done.4
  68.3 1.1 %constant_dynamic-update-slice_fusion.8 = bf16[32,128,256]{2,1,0:T(8,128)(2,1)S(1)} fusion(bf16[32,128,256]{2,1,0:T(8,128)(2,1)S(1)} %get-tuple-element.14, bf16[4,128,256]{2,1,0:T(8,128)(2,1)} %collective-permute-done.4), kind=kLoop, calls=%fused_computation.9 | loop fusion | bytes 524288
  69.5 0.0 collective-permute-done.5
  69.5 0.0 collective-permute-done.6
  69.5 1.1 %constant_dynamic-update-slice_fusion.6 = bf16[32,128,256]{2,1,0:T(8,128)(2,1)S(1)} fusion(bf16[32,128,256]{2,1,0:T(8,128)(2,1)S(1)} %constant_dynamic-update-slice_fusion.7, bf16[8,128,256]{2,1,0:T(8,128)(2,1)} %collective-permute-done.6), kind=kLoop, calls=%fused_computation.7 | loop fusion | bytes 1048576
  70.6 0.0 collective-permute-done.7
  70.7 0.0 copy-done.4
  70.7 0.0 copy-done.2
  70.7 0.0 copy-done.10
  70.7 20.0 %vert.1 = bf16[2048,512]{1,0:T(8,128)(2,1)} custom-call(s32[1]{0:T(128)} %bitcast.base_ref, bf16[2048,512]{1,0:T(8,128)(2,1)S(1)} %copy-done.2, bf16[32,128,256]{2,1,0:T(8,128)(2,1)S(1)} %constant_dynamic-update-slice_fusion.5.g_ref, s32[4,512]{1,0:T(4,128)S(1)} %copy-done.12, s32[512,4]{1,0:T(8,128)S(1)} %bitcast.6, s32[1,1024]{1,0:T(1,128)S(1)} %add.68.code_ref, ...), custom_call_target="tpu_custom_call" | custom-call | flops 2147483648 | bytes 12582912 | tf_op jit(solution)/shard_map/vert/pallas_call | solution.py:132
  (6 shorter events, 0.1 us)
Async XLA Ops:
  0.0 1.0 %copy-start.5 = (bf16[2048,128]{1,0:T(8,128)(2,1)S(1)}, bf16[2048,128]{1,0:T(8,128)(2,1)}, u32[]{:S(2)}) copy-start(bf16[2048,128]{1,0:T(8,128)(2,1)} %k1_ref.3) | copy-start | bytes 1572868
  1.0 1.0 %copy-start.7 = (bf16[2048,128]{1,0:T(8,128)(2,1)S(1)}, bf16[2048,128]{1,0:T(8,128)(2,1)}, u32[]{:S(2)}) copy-start(bf16[2048,128]{1,0:T(8,128)(2,1)} %v1_ref.3) | copy-start | bytes 1572868
  2.1 0.7 copy-start.11
  2.8 19.6 %copy-start.6 = (bf16[2048,128]{1,0:T(8,128)(2,1)S(1)}, bf16[2048,128]{1,0:T(8,128)(2,1)}, u32[]{:S(2)}) copy-start(bf16[2048,128]{1,0:T(8,128)(2,1)} %k1_ref.3) | copy-start | bytes 1572868
  2.8 19.6 %copy-start.8 = (bf16[2048,128]{1,0:T(8,128)(2,1)S(1)}, bf16[2048,128]{1,0:T(8,128)(2,1)}, u32[]{:S(2)}) copy-start(bf16[2048,128]{1,0:T(8,128)(2,1)} %v1_ref.3) | copy-start | bytes 1572868
  3.5 31.0 %collective-permute-start.2 = (bf16[1,128,256]{2,1,0:T(8,128)(2,1)S(1)}, bf16[1,128,256]{2,1,0:T(8,128)(2,1)S(1)}, u32[]{:S(2)}, u32[]{:S(2)}) collective-permute-start(bf16[1,128,256]{2,1,0:T(8,128)(2,1)S(1)} %bitcast.7), channel_id=1, source_target_pairs={{0,48},{1,17},{2,50},{3,19},{4,52},{5,21},{6,54},{7,23},{8,56},{9,... | collective-permute-start | bytes 196616 | tf_op jit(solution)/shard_map/ppermute | solution.py:160
  7.4 27.1 %collective-permute-start.1 = (bf16[1,128,256]{2,1,0:T(8,128)(2,1)S(1)}, bf16[1,128,256]{2,1,0:T(8,128)(2,1)S(1)}, u32[]{:S(2)}, u32[]{:S(2)}) collective-permute-start(bf16[1,128,256]{2,1,0:T(8,128)(2,1)S(1)} %bitcast.8), channel_id=1, source_target_pairs={{0,32},{1,33},{2,34},{3,35},{4,36},{5,37},{6,38},{7,39},{8,40},{9,... | collective-permute-start | bytes 196616 | tf_op jit(solution)/shard_map/ppermute | solution.py:160
  12.5 22.0 %collective-permute-start = (bf16[1,128,256]{2,1,0:T(8,128)(2,1)S(1)}, bf16[1,128,256]{2,1,0:T(8,128)(2,1)}, u32[]{:S(2)}, u32[]{:S(2)}) collective-permute-start(bf16[1,128,256]{2,1,0:T(8,128)(2,1)S(1)} %bitcast.9), channel_id=1, source_target_pairs={{0,16},{1,49},{2,18},{3,51},{4,20},{5,53},{6,22},{7,55},{8,24},{9,... | collective-permute-start | bytes 196616 | tf_op jit(solution)/shard_map/ppermute | solution.py:160
  15.6 39.1 %collective-permute-start.9 = (bf16[1024,128]{1,0:T(8,128)(2,1)}, bf16[1024,128]{1,0:T(8,128)(2,1)}, u32[]{:S(2)}, u32[]{:S(2)}) collective-permute-start(bf16[1024,128]{1,0:T(8,128)(2,1)} %slice.9), channel_id=1, source_target_pairs={{0,8},{8,16},{16,24},{24,32},{32,40},{40,48},{48,56},{56,64},{64,7... | collective-permute-start | bytes 786440 | tf_op jit(solution)/shard_map/ppermute | solution.py:191
  19.7 36.5 %collective-permute-start.8 = (bf16[1024,128]{1,0:T(8,128)(2,1)}, bf16[1024,128]{1,0:T(8,128)(2,1)}, u32[]{:S(2)}, u32[]{:S(2)}) collective-permute-start(bf16[1024,128]{1,0:T(8,128)(2,1)} %slice.8), channel_id=1, source_target_pairs={{0,8},{8,16},{16,24},{24,32},{32,40},{40,48},{48,56},{56,64},{64,7... | collective-permute-start | bytes 786440 | tf_op jit(solution)/shard_map/ppermute | solution.py:190
  22.3 1.6 %copy-start = (bf16[2048,512]{1,0:T(8,128)(2,1)S(1)}, bf16[2048,512]{1,0:T(8,128)(2,1)}, u32[]{:S(2)}) copy-start(bf16[2048,512]{1,0:T(8,128)(2,1)} %q_ref.5) | copy-start | bytes 6291460
  23.9 10.5 %copy-start.13 = (s32[32]{0:T(128)S(1)}, s32[32]{0:T(128)}, u32[]{:S(2)}) copy-start(s32[32]{0:T(128)} %constant.76.clone) | copy-start | bytes 388
  23.9 10.6 %copy-start.14 = (s32[32]{0:T(128)S(1)}, s32[32]{0:T(128)}, u32[]{:S(2)}) copy-start(s32[32]{0:T(128)} %constant.75.clone) | copy-start | bytes 388
  23.9 28.4 %copy-start.12 = (s32[4,512]{1,0:T(4,128)S(1)}, s32[4,512]{1,0:T(4,128)}, u32[]{:S(2)}) copy-start(s32[4,512]{1,0:T(4,128)} %vert_ref.3) | copy-start | bytes 24580
  33.2 1.3 %copy-start.3 = (f32[1024,512]{1,0:T(8,128)}, f32[1024,512]{1,0:T(8,128)S(1)}, u32[]{:S(2)}) copy-start(f32[1024,512]{1,0:T(8,128)S(1)} %get-tuple-element.11.a1_ref) | copy-start | bytes 6291460
  34.5 17.1 %copy-start.9 = (f32[1024,128]{1,0:T(8,128)}, f32[1024,128]{1,0:T(8,128)S(1)}, u32[]{:S(2)}) copy-start(f32[1024,128]{1,0:T(8,128)S(1)} %get-tuple-element.12.ml1_ref) | copy-start | bytes 1572868
  36.2 32.1 %collective-permute-start.4 = (bf16[4,128,256]{2,1,0:T(8,128)(2,1)}, bf16[4,128,256]{2,1,0:T(8,128)(2,1)}, u32[]{:S(2)}, u32[]{:S(2)}) collective-permute-start(bf16[4,128,256]{2,1,0:T(8,128)(2,1)} %pad_maximum_fusion), channel_id=1, source_target_pairs={{0,72},{1,249},{2,74},{3,251},{4,76},{5,253},{6,78},{7,255},{8,80}... | collective-permute-start | bytes 786440 | tf_op jit(solution)/shard_map/ppermute | solution.py:160
  36.2 14.7 %collective-permute-start.3 = (bf16[4,128,256]{2,1,0:T(8,128)(2,1)}, bf16[4,128,256]{2,1,0:T(8,128)(2,1)S(1)}, u32[]{:S(2)}, u32[]{:S(2)}) collective-permute-start(bf16[4,128,256]{2,1,0:T(8,128)(2,1)} %pad_maximum_fusion), channel_id=1, source_target_pairs={{0,128},{1,129},{2,130},{3,131},{4,132},{5,133},{6,134},{7,135},{8... | collective-permute-start | bytes 786440 | tf_op jit(solution)/shard_map/ppermute | solution.py:160
  51.6 17.9 %collective-permute-start.6 = (bf16[8,128,256]{2,1,0:T(8,128)(2,1)}, bf16[8,128,256]{2,1,0:T(8,128)(2,1)}, u32[]{:S(2)}, u32[]{:S(2)}) collective-permute-start(bf16[8,128,256]{2,1,0:T(8,128)(2,1)} %get-tuple-element.13), channel_id=1, source_target_pairs={{0,64},{1,193},{2,66},{3,195},{4,68},{5,197},{6,70},{7,199},{8,72}... | collective-permute-start | bytes 1572872 | tf_op jit(solution)/shard_map/ppermute | solution.py:160
  52.5 16.9 %collective-permute-start.5 = (bf16[4,128,256]{2,1,0:T(8,128)(2,1)}, bf16[4,128,256]{2,1,0:T(8,128)(2,1)S(1)}, u32[]{:S(2)}, u32[]{:S(2)}) collective-permute-start(bf16[4,128,256]{2,1,0:T(8,128)(2,1)} %pad_maximum_fusion), channel_id=1, source_target_pairs={{0,200},{1,121},{2,202},{3,123},{4,204},{5,125},{6,206},{7,127},{8... | collective-permute-start | bytes 786440 | tf_op jit(solution)/shard_map/ppermute | solution.py:160
  54.7 15.9 %collective-permute-start.7 = (bf16[8,128,256]{2,1,0:T(8,128)(2,1)}, bf16[8,128,256]{2,1,0:T(8,128)(2,1)S(1)}, u32[]{:S(2)}, u32[]{:S(2)}) collective-permute-start(bf16[8,128,256]{2,1,0:T(8,128)(2,1)} %get-tuple-element.13), channel_id=1, source_target_pairs={{0,8},{1,57},{2,10},{3,59},{4,12},{5,61},{6,14},{7,63},{8,16},{9,1... | collective-permute-start | bytes 1572872 | tf_op jit(solution)/shard_map/ppermute | solution.py:160
  56.2 1.6 %copy-start.1 = (bf16[2048,512]{1,0:T(8,128)(2,1)S(1)}, bf16[2048,512]{1,0:T(8,128)(2,1)}, u32[]{:S(2)}) copy-start(bf16[2048,512]{1,0:T(8,128)(2,1)} %q_ref.5) | copy-start | bytes 6291460
  57.8 12.9 %copy-start.4 = (f32[1024,512]{1,0:T(8,128)S(1)}, f32[1024,512]{1,0:T(8,128)}, u32[]{:S(2)}) copy-start(f32[1024,512]{1,0:T(8,128)} %copy-done.3) | copy-start | bytes 6291460
  68.3 2.4 %copy-start.2 = (bf16[2048,512]{1,0:T(8,128)(2,1)S(1)}, bf16[2048,512]{1,0:T(8,128)(2,1)}, u32[]{:S(2)}) copy-start(bf16[2048,512]{1,0:T(8,128)(2,1)} %q_ref.5) | copy-start | bytes 6291460
  68.3 2.4 %copy-start.10 = (f32[1024,128]{1,0:T(8,128)S(1)}, f32[1024,128]{1,0:T(8,128)}, u32[]{:S(2)}) copy-start(f32[1024,128]{1,0:T(8,128)} %copy-done.9) | copy-start | bytes 1572868

commit v2 on v0

v2 whole, which is shorter than its diff:
```python
import math

import jax
import jax.numpy as jnp
from jax import lax
from jax.experimental import pallas as pl
from jax.experimental.pallas import tpu as pltpu
from jax.sharding import PartitionSpec as P

TOK = 2048
HEAD = 128
GROUP = 4
COLS = 512
BAND = 1024
CAP = 32
NCTX = 32
QB = 256
VR = HEAD + 16
C = math.log2(math.e) / math.sqrt(HEAD)
F32 = jnp.float32
BF = jnp.bfloat16
NEG = -1e30
LIMIT = 56 << 20


def dot(a, b):
    return jnp.dot(a, b, preferred_element_type=F32)


def dot_t(a, b):
    return lax.dot_general(a, b, (((1,), (1,)), ((), ())), preferred_element_type=F32)


def pick_kernel(base_ref, vert_ref, k_ref, v_ref, out_ref, edge_ref):
    base = base_ref[0]
    vert = vert_ref[...]
    cols = lax.broadcasted_iota(jnp.int32, (CAP, COLS), 1)
    slot = lax.broadcasted_iota(jnp.int32, (CAP, COLS), 0)
    toks = lax.broadcasted_iota(jnp.int32, (CAP, TOK), 1)
    rows = []
    for h in range(GROUP):
        v = vert[h : h + 1, :] - base
        start = jnp.sum((v < 0).astype(jnp.int32), axis=1, keepdims=True)
        hit = (cols - start == slot) & (v < TOK)
        pos = jnp.sum(jnp.where(hit, v + 1, 0), axis=1, keepdims=True) - 1
        rows.append((toks == pos).astype(F32).astype(BF))
    sel = jnp.concatenate(rows, 0)
    out_ref[0, :, :HEAD] = dot(sel, k_ref[...]).astype(BF)
    out_ref[0, :, HEAD:] = dot(sel, v_ref[...]).astype(BF)
    edge_ref[:BAND, :] = k_ref[TOK - BAND :, :]
    edge_ref[BAND:, :] = v_ref[TOK - BAND :, :]


def pick(base, vertical, keys, values):
    full = lambda *s: pl.BlockSpec(s, lambda i: (0,) * len(s))
    return pl.pallas_call(
        pick_kernel,
        grid=(1,),
        out_shape=(
            jax.ShapeDtypeStruct((1, GROUP * CAP, 2 * HEAD), BF),
            jax.ShapeDtypeStruct((2 * BAND, HEAD), BF),
        ),
        in_specs=[pl.BlockSpec(memory_space=pltpu.SMEM), full(GROUP, COLS), full(TOK, HEAD), full(TOK, HEAD)],
        out_specs=(full(1, GROUP * CAP, 2 * HEAD), full(2 * BAND, HEAD)),
        compiler_params=pltpu.CompilerParams(vmem_limit_bytes=LIMIT),
        name="pick",
    )(base, vertical, keys, values)


def band_kernel(first_ref, q_ref, k0_ref, k1_ref, v0_ref, v1_ref, acc_ref, ml_ref, kx, vt):
    step = pl.program_id(0)

    @pl.when(step == 0)
    def _():
        first = first_ref[0] != 0
        kx[:BAND, :] = jnp.where(first, jnp.broadcast_to(k1_ref[0:1, :], k0_ref.shape), k0_ref[...])
        kx[BAND:, :] = k1_ref[...]
        vt[:HEAD, :BAND] = jnp.where(first, jnp.zeros(v0_ref.shape, BF), v0_ref[...]).T
        vt[:HEAD, BAND:] = v1_ref[...].T
        one = jnp.ones((VR - HEAD, BAND), BF)
        vt[HEAD:, :BAND] = jnp.where(first, jnp.zeros_like(one), one)
        vt[HEAD:, BAND:] = one

    off = pl.multiple_of(step * QB, QB)
    tri = lax.broadcasted_iota(jnp.int32, (QB, QB), 0) <= lax.broadcasted_iota(jnp.int32, (QB, QB), 1)
    scores = lambda h: dot_t(kx[pl.ds(off, BAND + QB), :], q_ref[:, h * HEAD : (h + 1) * HEAD])
    nxt = scores(0)
    for h in range(GROUP):
        s = nxt
        if h + 1 < GROUP:
            nxt = scores(h + 1)
        s_in = s[QB:BAND]
        s_edge = jnp.where(tri, s[BAND:], s[:QB])
        m = jnp.maximum(jnp.max(s_in, axis=0, keepdims=True), jnp.max(s_edge, axis=0, keepdims=True))
        p_in = jnp.exp2((s_in - m) * C).astype(BF)
        p_edge = jnp.exp2((s_edge - m) * C)
        p_last = jnp.where(tri, p_edge, 0.0).astype(BF)
        p_first = jnp.where(tri, 0.0, p_edge).astype(BF)
        p = jnp.concatenate([p_first, p_in, p_last], 0)
        o = dot(vt[:, pl.ds(off, BAND + QB)], p)
        acc_ref[h * HEAD : (h + 1) * HEAD, :] = o[:HEAD]
        ml_ref[h : h + 1, :] = m
        ml_ref[GROUP + h : GROUP + h + 1, :] = o[HEAD : HEAD + 1]


def band(first, queries, qhalf, k0, k1, v0, v1, bk0, bk1, bv0, bv1):
    n = BAND // QB
    spec = lambda b: pl.BlockSpec((BAND, HEAD), lambda i: (b, 0))
    return pl.pallas_call(
        band_kernel,
        grid=(n,),
        out_shape=(
            jax.ShapeDtypeStruct((GROUP * HEAD, BAND), F32),
            jax.ShapeDtypeStruct((2 * GROUP, BAND), F32),
        ),
        in_specs=[
            pl.BlockSpec(memory_space=pltpu.SMEM),
            pl.BlockSpec((QB, GROUP * HEAD), lambda i: (qhalf * n + i, 0)),
            spec(bk0),
            spec(bk1),
            spec(bv0),
            spec(bv1),
        ],
        out_specs=(
            pl.BlockSpec((GROUP * HEAD, QB), lambda i: (0, i)),
            pl.BlockSpec((2 * GROUP, QB), lambda i: (0, i)),
        ),
        scratch_shapes=[pltpu.VMEM((2 * BAND, HEAD), BF), pltpu.VMEM((VR, 2 * BAND), BF)],
        compiler_params=pltpu.CompilerParams(vmem_limit_bytes=LIMIT),
        cost_estimate=pl.CostEstimate(
            flops=8 * BAND * GROUP * HEAD * (BAND + QB),
            bytes_accessed=5 << 20,
            transcendentals=BAND * BAND * GROUP,
        ),
        name="band",
    )(first, queries, k0, k1, v0, v1)


def vert_kernel(nparts, *refs):
    base_ref, q_ref = refs[:2]
    g_refs = refs[2 : 2 + nparts]
    vertt_ref, code_ref, a0_ref, ml0_ref, a1_ref, ml1_ref, out_ref, kx, vt = refs[2 + nparts :]
    step = pl.program_id(0)

    @pl.when(step == 0)
    def _():
        lanes = lax.broadcasted_iota(jnp.int32, (COLS, HEAD), 1)
        rows = lax.broadcasted_iota(jnp.int32, (COLS, 1), 0)
        for h in range(GROUP):
            v = vertt_ref[:, h : h + 1]
            starts = jnp.sum((v < lanes * TOK).astype(jnp.int32), axis=0, keepdims=True)
            d = v // TOK
            start = jnp.sum(jnp.where(lanes == d, starts, 0), axis=1, keepdims=True)
            mine = d * CAP + rows - start
            t = None
            at = 0
            for g in g_refs:
                n = g.shape[0] * CAP
                sel = (mine == code_ref[:, at : at + n]).astype(F32).astype(BF)
                at += n
                part = dot(sel, g[:, h * CAP : (h + 1) * CAP, :].reshape(n, 2 * HEAD))
                t = part if t is None else t + part
            kx[h] = t[:, :HEAD].astype(BF)
            vt[h, :HEAD, :] = t[:, HEAD:].astype(BF).T
            vt[h, HEAD:, :] = jnp.ones((VR - HEAD, COLS), BF)

    half = (TOK // QB) // 2
    qpos = base_ref[0] + step * QB - BAND + lax.broadcasted_iota(jnp.int32, (1, QB), 1)

    def body(a_ref, ml_ref):
        scores = lambda h: dot_t(kx[h], q_ref[:, h * HEAD : (h + 1) * HEAD])
        nxt = scores(0)
        for h in range(GROUP):
            s = nxt
            if h + 1 < GROUP:
                nxt = scores(h + 1)
            s = jnp.where(vertt_ref[:, h : h + 1] <= qpos, s, NEG)
            mb = ml_ref[h : h + 1, :]
            lb = ml_ref[GROUP + h : GROUP + h + 1, :]
            m = jnp.maximum(jnp.max(s, axis=0, keepdims=True), mb)
            p = jnp.exp2((s - m) * C).astype(BF)
            o = dot(vt[h], p)
            alpha = jnp.exp2((mb - m) * C)
            den = o[HEAD : HEAD + 1] + lb * alpha
            num = a_ref[h * HEAD : (h + 1) * HEAD, :] * alpha + o[:HEAD]
            out_ref[:, h * HEAD : (h + 1) * HEAD] = (num * (1.0 / den)).T.astype(BF)

    @pl.when(step < half)
    def _():
        body(a0_ref, ml0_ref)

    @pl.when(step >= half)
    def _():
        body(a1_ref, ml1_ref)


def vert(base, queries, parts, vertt, code, a0, ml0, a1, ml1):
    n = TOK // QB
    full = lambda *s: pl.BlockSpec(s, lambda i: (0,) * len(s))
    lo = lambda i: (0, jnp.minimum(i, n // 2 - 1))
    hi = lambda i: (0, jnp.maximum(i - n // 2, 0))
    return pl.pallas_call(
        lambda *refs: vert_kernel(len(parts), *refs),
        grid=(n,),
        out_shape=jax.ShapeDtypeStruct((TOK, GROUP * HEAD), BF),
        in_specs=[
            pl.BlockSpec(memory_space=pltpu.SMEM),
            pl.BlockSpec((QB, GROUP * HEAD), lambda i: (i, 0)),
            *[full(*p.shape) for p in parts],
            full(COLS, GROUP),
            full(1, NCTX * CAP),
            pl.BlockSpec((GROUP * HEAD, QB), lo),
            pl.BlockSpec((2 * GROUP, QB), lo),
            pl.BlockSpec((GROUP * HEAD, QB), hi),
            pl.BlockSpec((2 * GROUP, QB), hi),
        ],
        out_specs=pl.BlockSpec((QB, GROUP * HEAD), lambda i: (i, 0)),
        scratch_shapes=[pltpu.VMEM((GROUP, COLS, HEAD), BF), pltpu.VMEM((GROUP, VR, COLS), BF)],
        compiler_params=pltpu.CompilerParams(vmem_limit_bytes=LIMIT),
        cost_estimate=pl.CostEstimate(
            flops=8 * TOK * GROUP * HEAD * COLS,
            bytes_accessed=12 << 20,
            transcendentals=TOK * COLS * GROUP,
        ),
        name="vert",
    )(base, queries, *parts, vertt, code, a0, ml0, a1, ml1)


AXES = ("ctx", "kvh")


def hop(array, grid, step):
    ny, nz = grid
    nk = lax.axis_size("kvh")
    pairs = []
    for y in range(ny):
        for z in range(nz):
            for k in range(nk):
                s = 1 if k % 2 == 0 else -1
                to = ((y + s * step[0]) % ny) * nz + (z + s * step[1]) % nz
                pairs.append(((y * nz + z) * nk + k, to * nk + k))
    return lax.ppermute(array, AXES, pairs)


def shifted(came, step):
    return [(y - step[0], z - step[1]) for y, z in came]


def spread(own):
    grid = (4, 8)
    steps = ((0, 2), (0, 4), (0, -2))
    four = jnp.concatenate([own] + [hop(own, grid, s) for s in steps], 0)
    came4 = [(0, 0)] + [shifted([(0, 0)], s)[0] for s in steps]
    far, left, right = (2, 0), (1, 1), (-1, 1)
    even = jnp.concatenate([four, hop(four, grid, far)], 0)
    came8 = came4 + shifted(came4, far)
    parts = [even, hop(four, grid, left), hop(four, grid, right), hop(even, grid, (1, 0)), hop(even, grid, (0, 1))]
    came = came8 + shifted(came4, left) + shifted(came4, right) + shifted(came8, (1, 0)) + shifted(came8, (0, 1))
    return parts, came


def shards(queries, keys, values, vertical):
    ctx = lax.axis_index("ctx")
    base = (ctx * TOK).astype(jnp.int32)[None]
    inner = jnp.zeros((1,), jnp.int32)
    first = (ctx == 0).astype(jnp.int32)[None]

    own, edge = pick(base, vertical, keys, values)
    edge = lax.ppermute(edge, "ctx", [(i, i + 1) for i in range(NCTX - 1)])
    parts, came = spread(own)

    sign = 1 - 2 * (lax.axis_index("kvh") % 2)
    oy = jnp.asarray([o[0] for o in came], jnp.int32)
    oz = jnp.asarray([o[1] for o in came], jnp.int32)
    device = ((ctx // 8 + sign * oy) % 4) * 8 + (ctx % 8 + sign * oz) % 8
    code = (device[:, None] * CAP + jnp.arange(CAP, dtype=jnp.int32)[None, :]).reshape(1, -1)

    acc1, ml1 = band(inner, queries, 1, keys, keys, values, values, 0, 1, 0, 1)
    acc0, ml0 = band(first, queries, 0, edge, keys, edge, values, 0, 0, 1, 0)
    return vert(base, queries, parts, vertical.T, code, acc0, ml0, acc1, ml1)


def solution(mesh):
    in_specs = (P("ctx", "kvh"), P("ctx", "kvh"), P("ctx", "kvh"), P("kvh", None))
    return jax.shard_map(shards, mesh=mesh, in_specs=in_specs, out_specs=P("ctx", "kvh"), check_vma=False)
```

time: 277 us -> 71.6 us (0.26)
  the two profiles are of different devices: /device:TPU:1 before, /device:TPU:8 now
where the time goes in v2:
time: 71.6 us; the launch traced here: 71.3 us
  Pallas kernels  39.1 us (55%)
  starting transfers between devices  23.3 us (33%)
  waiting for transfers between devices  4.4 us (6%)
  local copies, waits for them, and re-layouts  4.28 us (6%)
    pallas_call x2, Pallas kernels, band(): pl.pallas_call(band_kernel, grid=(n,), out_shape=(jax.ShapeDtypeStruct((G...  20.5 us
    ppermute x8, starting transfers between devices, hop(): return lax.ppermute(array, AXES, pairs)  20.4 us
    pallas_call x1, Pallas kernels, vert(): pl.pallas_call(lambda *refs: vert_kernel(len(parts), *refs), grid=(n,), o...  16 us
    ppermute x8, waiting for transfers between devices, hop(): return lax.ppermute(array, AXES, pairs)  4.4 us
    unnamed x22, local copies, waits for them, and re-layouts  3.58 us
    ppermute x1, starting transfers between devices, shards(): edge = lax.ppermute(edge, 'ctx', [(i, i + 1) for i in range(NCTX - 1)])  2.92 us
    pallas_call x1, Pallas kernels, pick(): pl.pallas_call(pick_kernel, grid=(1,), out_shape=(jax.ShapeDtypeStruct((1...  2.65 us
  transfers between devices with their start and end apart: 9, of which 3 were waited for; matrix products, arithmetic and copies ran while one was open for 4% of the time, Pallas kernels for 29%

profile of v2, /device:TPU:8, one launch (start us, length us, event | category | flops | bytes accessed | tf_op | source)
XLA Modules:
  0.0 71.3 jit_solution(14043942630307214569)
XLA Ops:
  0.0 2.7 %pick.1 = (bf16[1,128,256]{2,1,0:T(8,128)(2,1)}, bf16[2048,128]{1,0:T(8,128)(2,1)}) custom-call(s32[1]{0:T(128)} %bitcast.base_ref.refs_0_, s32[4,512]{1,0:T(4,128)} %vert_ref.1, bf16[2048,128]{1,0:T(8,128)(2,1)} %k1_ref.3, bf16[2048,128]{1,0:T(8,128)(2,1)} %v1_ref.3), custom_call_target="tpu_custom_call" | custom-call | tf_op jit(solution)/shard_map/pick/pallas_call | solution.py:56
  2.7 6.3 %collective-permute-start.2 = (bf16[1,128,256]{2,1,0:T(8,128)(2,1)}, bf16[1,128,256]{2,1,0:T(8,128)(2,1)S(1)}, u32[]{:S(2)}, u32[]{:S(2)}) collective-permute-start(bf16[1,128,256]{2,1,0:T(8,128)(2,1)} %get-tuple-element.11), channel_id=1, source_target_pairs={{0,48},{1,17},{2,50},{3,19},{4,52},{5,21},{6,54},{7,23},{8,56},{9,... | collective-permute-start | bytes 196616 | tf_op jit(solution)/shard_map/ppermute | solution.py:242
  9.0 0.9 %collective-permute-start.1 = (bf16[1,128,256]{2,1,0:T(8,128)(2,1)}, bf16[1,128,256]{2,1,0:T(8,128)(2,1)S(1)}, u32[]{:S(2)}, u32[]{:S(2)}) collective-permute-start(bf16[1,128,256]{2,1,0:T(8,128)(2,1)} %get-tuple-element.11), channel_id=1, source_target_pairs={{0,32},{1,33},{2,34},{3,35},{4,36},{5,37},{6,38},{7,39},{8,40},{9,... | collective-permute-start | bytes 196616 | tf_op jit(solution)/shard_map/ppermute | solution.py:242
  9.8 2.9 %collective-permute-start = (bf16[1,128,256]{2,1,0:T(8,128)(2,1)}, bf16[1,128,256]{2,1,0:T(8,128)(2,1)S(1)}, u32[]{:S(2)}, u32[]{:S(2)}) collective-permute-start(bf16[1,128,256]{2,1,0:T(8,128)(2,1)} %get-tuple-element.11), channel_id=1, source_target_pairs={{0,16},{1,49},{2,18},{3,51},{4,20},{5,53},{6,22},{7,55},{8,24},{9,... | collective-permute-start | bytes 196616 | tf_op jit(solution)/shard_map/ppermute | solution.py:242
  12.8 2.9 %collective-permute-start.8 = (bf16[2048,128]{1,0:T(8,128)(2,1)}, bf16[2048,128]{1,0:T(8,128)(2,1)S(1)}, u32[]{:S(2)}, u32[]{:S(2)}) collective-permute-start(bf16[2048,128]{1,0:T(8,128)(2,1)} %get-tuple-element.12), channel_id=1, source_target_pairs={{0,8},{8,16},{16,24},{24,32},{32,40},{40,48},{48,56},{56,64},{64,7... | collective-permute-start | bytes 1572872 | tf_op jit(solution)/shard_map/ppermute | solution.py:269
  15.7 0.8 %constant_dynamic-update-slice_fusion.3 = (bf16[4,128,256]{2,1,0:T(8,128)(2,1)S(1)}, bf16[8,128,256]{2,1,0:T(8,128)(2,1)S(1)}) fusion(bf16[1,128,256]{2,1,0:T(8,128)(2,1)} %get-tuple-element.11), kind=kLoop, calls=%fused_computation.3 | loop fusion | bytes 196608
  16.5 1.2 %collective-permute-done = bf16[1,128,256]{2,1,0:T(8,128)(2,1)S(1)} collective-permute-done((bf16[1,128,256]{2,1,0:T(8,128)(2,1)}, bf16[1,128,256]{2,1,0:T(8,128)(2,1)S(1)}, u32[]{:S(2)}, u32[]{:S(2)}) %collective-permute-start) | collective-permute-done | bytes 65568 | tf_op jit(solution)/shard_map/ppermute | solution.py:242
  17.7 0.0 collective-permute-done.1
  17.8 0.0 collective-permute-done.2
  17.8 0.0 copy-start.2
  17.8 0.0 copy-start.3
  17.8 0.0 copy-start
  17.8 2.4 %collective-permute-start.3 = (bf16[4,128,256]{2,1,0:T(8,128)(2,1)S(1)}, bf16[4,128,256]{2,1,0:T(8,128)(2,1)S(1)}, u32[]{:S(2)}, u32[]{:S(2)}) collective-permute-start(bf16[4,128,256]{2,1,0:T(8,128)(2,1)S(1)} %get-tuple-element.17), channel_id=1, source_target_pairs={{0,128},{1,129},{2,130},{3,131},{4,132},{5,133},{6,134},{7,135},{8... | collective-permute-start | bytes 786440 | tf_op jit(solution)/shard_map/ppermute | solution.py:242
  20.2 10.2 %band.3 = (f32[512,1024]{1,0:T(8,128)}, f32[8,1024]{1,0:T(8,128)}) custom-call(s32[1]{0:T(128)} %constant.74.clone.1.first_ref, bf16[2048,512]{1,0:T(8,128)(2,1)} %refs_1_.1, bf16[2048,128]{1,0:T(8,128)(2,1)} %k1_ref.3, bf16[2048,128]{1,0:T(8,128)(2,1)} %k1_ref.3, bf16[2048,128]{1,0:T(8,128)(2,1)} %v1_ref.3, bf16[2048,128]{1,0:T(8,128)(2,1)} %v1_ref.3), custom_call_target="tpu_custom_call" | custom-call | flops 5368709120 | bytes 5242880 | tf_op jit(solution)/shard_map/band/pallas_call | solution.py:109
  30.5 0.0 copy-done.2
  30.5 0.0 copy-done.3
  30.5 0.0 collective-permute-done.3
  30.5 0.0 copy-start.1
  30.5 1.8 %collective-permute-start.7 = (bf16[8,128,256]{2,1,0:T(8,128)(2,1)S(1)}, bf16[8,128,256]{2,1,0:T(8,128)(2,1)S(1)}, u32[]{:S(2)}, u32[]{:S(2)}) collective-permute-start(bf16[8,128,256]{2,1,0:T(8,128)(2,1)S(1)} %constant_dynamic-update-slice_fusion.4.refs_2_), channel_id=1, source_target_pairs={{0,8},{1,57},{2,10},{3,59},{4,12},{5,61},{6,14},{7,63},{8,16},{9,1... | collective-permute-start | bytes 1572872 | tf_op jit(solution)/shard_map/ppermute | solution.py:242
  32.3 6.1 %collective-permute-start.6 = (bf16[8,128,256]{2,1,0:T(8,128)(2,1)S(1)}, bf16[8,128,256]{2,1,0:T(8,128)(2,1)S(1)}, u32[]{:S(2)}, u32[]{:S(2)}) collective-permute-start(bf16[8,128,256]{2,1,0:T(8,128)(2,1)S(1)} %constant_dynamic-update-slice_fusion.4.refs_2_), channel_id=1, source_target_pairs={{0,64},{1,193},{2,66},{3,195},{4,68},{5,197},{6,70},{7,199},{8,72}... | collective-permute-start | bytes 1572872 | tf_op jit(solution)/shard_map/ppermute | solution.py:242
  38.4 0.1 iota_add_fusion
  38.5 0.0 copy-done
  38.5 0.9 %copy.7 = s32[4,512]{0,1:T(8,128)} copy(s32[4,512]{1,0:T(4,128)S(1)} %copy-done) | data formatting | bytes 16384 | tf_op args[3]
  39.3 0.7 add.68.refs_8_
  40.0 0.0 collective-permute-start.5
  40.0 0.0 collective-permute-start.4
  40.0 0.0 collective-permute-done.8.k0_ref.v0_ref
  40.0 0.0 copy-start.4
  40.0 0.8 %copy-done.4 = bf16[2048,128]{1,0:T(8,128)(2,1)} copy-done((bf16[2048,128]{1,0:T(8,128)(2,1)}, bf16[2048,128]{1,0:T(8,128)(2,1)S(1)}, u32[]{:S(2)}) %copy-start.4) | copy-done | bytes 524312
  40.8 10.3 %band.2 = (f32[512,1024]{1,0:T(8,128)}, f32[8,1024]{1,0:T(8,128)}) custom-call(s32[1]{0:T(128)} %bitcast.2.first_ref, bf16[2048,512]{1,0:T(8,128)(2,1)} %refs_1_.1, bf16[2048,128]{1,0:T(8,128)(2,1)} %copy-done.4, bf16[2048,128]{1,0:T(8,128)(2,1)} %k1_ref.3, bf16[2048,128]{1,0:T(8,128)(2,1)} %copy-done.4, bf16[2048,128]{1,0:T(8,128)(2,1)} %v1_ref.3), custom_call_target="tpu_custom_call" | custom-call | flops 5368709120 | bytes 5242880 | tf_op jit(solution)/shard_map/band/pallas_call | solution.py:109
  51.1 0.0 copy-done.1
  51.1 1.5 %collective-permute-done.5.refs_4_ = bf16[4,128,256]{2,1,0:T(8,128)(2,1)S(1)} collective-permute-done((bf16[4,128,256]{2,1,0:T(8,128)(2,1)S(1)}, bf16[4,128,256]{2,1,0:T(8,128)(2,1)S(1)}, u32[]{:S(2)}, u32[]{:S(2)}) %collective-permute-start.5) | collective-permute-done | bytes 262176 | tf_op jit(solution)/shard_map/ppermute | solution.py:242
  52.6 0.0 copy-start.7
  52.6 1.7 %collective-permute-done.4.refs_3_ = bf16[4,128,256]{2,1,0:T(8,128)(2,1)S(1)} collective-permute-done((bf16[4,128,256]{2,1,0:T(8,128)(2,1)S(1)}, bf16[4,128,256]{2,1,0:T(8,128)(2,1)S(1)}, u32[]{:S(2)}, u32[]{:S(2)}) %collective-permute-start.4) | collective-permute-done | bytes 262176 | tf_op jit(solution)/shard_map/ppermute | solution.py:242
  54.3 0.0 copy-start.8
  54.3 0.0 collective-permute-done.7.refs_6_
  54.3 0.0 copy-start.5
  54.3 0.0 collective-permute-done.6.refs_5_
  54.3 0.0 copy-start.6
  54.3 0.0 copy-done.7
  54.3 0.7 copy-done.8
  55.0 0.2 copy-done.5
  55.2 0.2 copy-done.6
  55.4 16.0 %vert.1 = bf16[2048,512]{1,0:T(8,128)(2,1)} custom-call(s32[1]{0:T(128)} %bitcast.base_ref.refs_0_, bf16[2048,512]{1,0:T(8,128)(2,1)} %refs_1_.1, bf16[8,128,256]{2,1,0:T(8,128)(2,1)} %copy-done.1, bf16[4,128,256]{2,1,0:T(8,128)(2,1)} %copy-done.8, bf16[4,128,256]{2,1,0:T(8,128)(2,1)} %copy-done.7, bf16[8,128,256]{2,1,0:T(8,128)(2,1)} %copy-done.6, ...), custom_call_target="tpu_custom_call" | custom-call | flops 4294967296 | bytes 12582912 | tf_op jit(solution)/shard_map/vert/pallas_call | solution.py:202
  (5 shorter events, 0.1 us)
Async XLA Ops:
  2.7 15.1 %collective-permute-start.2 = (bf16[1,128,256]{2,1,0:T(8,128)(2,1)}, bf16[1,128,256]{2,1,0:T(8,128)(2,1)S(1)}, u32[]{:S(2)}, u32[]{:S(2)}) collective-permute-start(bf16[1,128,256]{2,1,0:T(8,128)(2,1)} %get-tuple-element.11), channel_id=1, source_target_pairs={{0,48},{1,17},{2,50},{3,19},{4,52},{5,21},{6,54},{7,23},{8,56},{9,... | collective-permute-start | bytes 196616 | tf_op jit(solution)/shard_map/ppermute | solution.py:242
  9.0 8.8 %collective-permute-start.1 = (bf16[1,128,256]{2,1,0:T(8,128)(2,1)}, bf16[1,128,256]{2,1,0:T(8,128)(2,1)S(1)}, u32[]{:S(2)}, u32[]{:S(2)}) collective-permute-start(bf16[1,128,256]{2,1,0:T(8,128)(2,1)} %get-tuple-element.11), channel_id=1, source_target_pairs={{0,32},{1,33},{2,34},{3,35},{4,36},{5,37},{6,38},{7,39},{8,40},{9,... | collective-permute-start | bytes 196616 | tf_op jit(solution)/shard_map/ppermute | solution.py:242
  9.8 7.9 %collective-permute-start = (bf16[1,128,256]{2,1,0:T(8,128)(2,1)}, bf16[1,128,256]{2,1,0:T(8,128)(2,1)S(1)}, u32[]{:S(2)}, u32[]{:S(2)}) collective-permute-start(bf16[1,128,256]{2,1,0:T(8,128)(2,1)} %get-tuple-element.11), channel_id=1, source_target_pairs={{0,16},{1,49},{2,18},{3,51},{4,20},{5,53},{6,22},{7,55},{8,24},{9,... | collective-permute-start | bytes 196616 | tf_op jit(solution)/shard_map/ppermute | solution.py:242
  12.8 27.2 %collective-permute-start.8 = (bf16[2048,128]{1,0:T(8,128)(2,1)}, bf16[2048,128]{1,0:T(8,128)(2,1)S(1)}, u32[]{:S(2)}, u32[]{:S(2)}) collective-permute-start(bf16[2048,128]{1,0:T(8,128)(2,1)} %get-tuple-element.12), channel_id=1, source_target_pairs={{0,8},{8,16},{16,24},{24,32},{32,40},{40,48},{48,56},{56,64},{64,7... | collective-permute-start | bytes 1572872 | tf_op jit(solution)/shard_map/ppermute | solution.py:269
  17.8 12.7 %copy-start.2 = (s32[32]{0:T(128)S(1)}, s32[32]{0:T(128)}, u32[]{:S(2)}) copy-start(s32[32]{0:T(128)} %constant.76.clone) | copy-start | bytes 388
  17.8 12.7 %copy-start.3 = (s32[32]{0:T(128)S(1)}, s32[32]{0:T(128)}, u32[]{:S(2)}) copy-start(s32[32]{0:T(128)} %constant.75.clone) | copy-start | bytes 388
  17.8 20.7 %copy-start = (s32[4,512]{1,0:T(4,128)S(1)}, s32[4,512]{1,0:T(4,128)}, u32[]{:S(2)}) copy-start(s32[4,512]{1,0:T(4,128)} %vert_ref.1) | copy-start | bytes 24580
  17.8 12.7 %collective-permute-start.3 = (bf16[4,128,256]{2,1,0:T(8,128)(2,1)S(1)}, bf16[4,128,256]{2,1,0:T(8,128)(2,1)S(1)}, u32[]{:S(2)}, u32[]{:S(2)}) collective-permute-start(bf16[4,128,256]{2,1,0:T(8,128)(2,1)S(1)} %get-tuple-element.17), channel_id=1, source_target_pairs={{0,128},{1,129},{2,130},{3,131},{4,132},{5,133},{6,134},{7,135},{8... | collective-permute-start | bytes 786440 | tf_op jit(solution)/shard_map/ppermute | solution.py:242
  30.5 20.5 %copy-start.1 = (bf16[8,128,256]{2,1,0:T(8,128)(2,1)}, bf16[8,128,256]{2,1,0:T(8,128)(2,1)S(1)}, u32[]{:S(2)}) copy-start(bf16[8,128,256]{2,1,0:T(8,128)(2,1)S(1)} %constant_dynamic-update-slice_fusion.4.refs_2_) | copy-start | bytes 1572868
  30.5 23.8 %collective-permute-start.7 = (bf16[8,128,256]{2,1,0:T(8,128)(2,1)S(1)}, bf16[8,128,256]{2,1,0:T(8,128)(2,1)S(1)}, u32[]{:S(2)}, u32[]{:S(2)}) collective-permute-start(bf16[8,128,256]{2,1,0:T(8,128)(2,1)S(1)} %constant_dynamic-update-slice_fusion.4.refs_2_), channel_id=1, source_target_pairs={{0,8},{1,57},{2,10},{3,59},{4,12},{5,61},{6,14},{7,63},{8,16},{9,1... | collective-permute-start | bytes 1572872 | tf_op jit(solution)/shard_map/ppermute | solution.py:242
  32.3 22.0 %collective-permute-start.6 = (bf16[8,128,256]{2,1,0:T(8,128)(2,1)S(1)}, bf16[8,128,256]{2,1,0:T(8,128)(2,1)S(1)}, u32[]{:S(2)}, u32[]{:S(2)}) collective-permute-start(bf16[8,128,256]{2,1,0:T(8,128)(2,1)S(1)} %constant_dynamic-update-slice_fusion.4.refs_2_), channel_id=1, source_target_pairs={{0,64},{1,193},{2,66},{3,195},{4,68},{5,197},{6,70},{7,199},{8,72}... | collective-permute-start | bytes 1572872 | tf_op jit(solution)/shard_map/ppermute | solution.py:242
  40.0 12.6 %collective-permute-start.5 = (bf16[4,128,256]{2,1,0:T(8,128)(2,1)S(1)}, bf16[4,128,256]{2,1,0:T(8,128)(2,1)S(1)}, u32[]{:S(2)}, u32[]{:S(2)}) collective-permute-start(bf16[4,128,256]{2,1,0:T(8,128)(2,1)S(1)} %get-tuple-element.17), channel_id=1, source_target_pairs={{0,200},{1,121},{2,202},{3,123},{4,204},{5,125},{6,206},{7,127},{8... | collective-permute-start | bytes 786440 | tf_op jit(solution)/shard_map/ppermute | solution.py:242
  40.0 14.3 %collective-permute-start.4 = (bf16[4,128,256]{2,1,0:T(8,128)(2,1)S(1)}, bf16[4,128,256]{2,1,0:T(8,128)(2,1)S(1)}, u32[]{:S(2)}, u32[]{:S(2)}) collective-permute-start(bf16[4,128,256]{2,1,0:T(8,128)(2,1)S(1)} %get-tuple-element.17), channel_id=1, source_target_pairs={{0,72},{1,249},{2,74},{3,251},{4,76},{5,253},{6,78},{7,255},{8,80}... | collective-permute-start | bytes 786440 | tf_op jit(solution)/shard_map/ppermute | solution.py:242
  40.0 0.8 %copy-start.4 = (bf16[2048,128]{1,0:T(8,128)(2,1)}, bf16[2048,128]{1,0:T(8,128)(2,1)S(1)}, u32[]{:S(2)}) copy-start(bf16[2048,128]{1,0:T(8,128)(2,1)S(1)} %collective-permute-done.8.k0_ref.v0_ref) | copy-start | bytes 1572868
  52.6 1.8 %copy-start.7 = (bf16[4,128,256]{2,1,0:T(8,128)(2,1)}, bf16[4,128,256]{2,1,0:T(8,128)(2,1)S(1)}, u32[]{:S(2)}) copy-start(bf16[4,128,256]{2,1,0:T(8,128)(2,1)S(1)} %collective-permute-done.5.refs_4_) | copy-start | bytes 786436
  54.3 0.7 copy-start.8
  54.3 0.9 %copy-start.5 = (bf16[8,128,256]{2,1,0:T(8,128)(2,1)}, bf16[8,128,256]{2,1,0:T(8,128)(2,1)S(1)}, u32[]{:S(2)}) copy-start(bf16[8,128,256]{2,1,0:T(8,128)(2,1)S(1)} %collective-permute-done.7.refs_6_) | copy-start | bytes 1572868
  54.3 1.1 %copy-start.6 = (bf16[8,128,256]{2,1,0:T(8,128)(2,1)}, bf16[8,128,256]{2,1,0:T(8,128)(2,1)S(1)}, u32[]{:S(2)}) copy-start(bf16[8,128,256]{2,1,0:T(8,128)(2,1)S(1)} %collective-permute-done.6.refs_5_) | copy-start | bytes 1572868

commit v3 on v2

v3 whole, which is shorter than its diff:
```python
import math

import jax
import jax.numpy as jnp
from jax import lax
from jax.experimental import pallas as pl
from jax.experimental.pallas import tpu as pltpu
from jax.sharding import PartitionSpec as P

TOK = 2048
HEAD = 128
GROUP = 4
COLS = 512
BAND = 1024
CAP = 32
NCTX = 32
QB = 256
VR = HEAD + 16
C = math.log2(math.e) / math.sqrt(HEAD)
F32 = jnp.float32
BF = jnp.bfloat16
NEG = -1e30
LIMIT = 56 << 20
VERT_LIMIT = 56 << 20
PIECE = 512
QV = 512
TINY = 2.0**-60
HUGE = 2.0**100


def dot(a, b):
    return jnp.dot(a, b, preferred_element_type=F32)


def dot_t(a, b):
    return lax.dot_general(a, b, (((1,), (1,)), ((), ())), preferred_element_type=F32)


def pick_kernel(base_ref, vert_ref, k_ref, v_ref, out_ref, edge_ref):
    base = base_ref[0]
    vert = vert_ref[...]
    cols = lax.broadcasted_iota(jnp.int32, (CAP, COLS), 1)
    slot = lax.broadcasted_iota(jnp.int32, (CAP, COLS), 0)
    toks = lax.broadcasted_iota(jnp.int32, (CAP, TOK), 1)
    rows = []
    for h in range(GROUP):
        v = vert[h : h + 1, :] - base
        start = jnp.sum((v < 0).astype(jnp.int32), axis=1, keepdims=True)
        hit = (cols - start == slot) & (v < TOK)
        pos = jnp.sum(jnp.where(hit, v + 1, 0), axis=1, keepdims=True) - 1
        rows.append((toks == pos).astype(F32).astype(BF))
    sel = jnp.concatenate(rows, 0)
    out_ref[0, :, :HEAD] = dot(sel, k_ref[...]).astype(BF)
    out_ref[0, :, HEAD:] = dot(sel, v_ref[...]).astype(BF)
    edge_ref[:BAND, :] = k_ref[TOK - BAND :, :]
    edge_ref[BAND:, :] = v_ref[TOK - BAND :, :]


def pick(base, vertical, keys, values):
    full = lambda *s: pl.BlockSpec(s, lambda i: (0,) * len(s))
    return pl.pallas_call(
        pick_kernel,
        grid=(1,),
        out_shape=(
            jax.ShapeDtypeStruct((1, GROUP * CAP, 2 * HEAD), BF),
            jax.ShapeDtypeStruct((2 * BAND, HEAD), BF),
        ),
        in_specs=[pl.BlockSpec(memory_space=pltpu.SMEM), full(GROUP, COLS), full(TOK, HEAD), full(TOK, HEAD)],
        out_specs=(full(1, GROUP * CAP, 2 * HEAD), full(2 * BAND, HEAD)),
        compiler_params=pltpu.CompilerParams(vmem_limit_bytes=LIMIT),
        name="pick",
    )(base, vertical, keys, values)


def plan_kernel(came, place_ref, vert_ref, cols_ref, code_ref):
    place = place_ref[0]
    y, z, core = place >> 4, (place >> 1) & 7, place & 1
    wide = jnp.concatenate([vert_ref[...].astype(F32), jnp.zeros((8 - GROUP, COLS), F32)], 0)
    cols = wide.T.astype(jnp.int32)
    lanes = lax.broadcasted_iota(jnp.int32, (COLS, HEAD), 1)
    rows = lax.broadcasted_iota(jnp.int32, (COLS, 1), 0)
    lane8 = lax.broadcasted_iota(jnp.int32, (COLS, 8), 1)
    out = cols
    for h in range(GROUP):
        v = cols[:, h : h + 1]
        starts = jnp.sum((v < lanes * TOK).astype(jnp.int32), axis=0, keepdims=True)
        d = v >> 11
        start = jnp.sum(jnp.where(lanes == d, starts, 0), axis=1, keepdims=True)
        out = jnp.where(lane8 == GROUP + h, d * CAP + rows - start, out)
    cols_ref[...] = out
    slot = lax.broadcasted_iota(jnp.int32, (1, NCTX * CAP), 1)
    block, within = slot >> 5, slot & (CAP - 1)
    code = within
    for n, (a, b) in enumerate(zip(*came)):
        dy = jnp.where(core == 0, a[0], b[0])
        dz = jnp.where(core == 0, a[1], b[1])
        device = ((y + dy) & 3) * 8 + ((z + dz) & 7)
        code = jnp.where(block == n, within + device * CAP, code)
    code_ref[...] = code


def plan(came, place, vertical):
    full = lambda *s: pl.BlockSpec(s, lambda i: (0,) * len(s))
    return pl.pallas_call(
        lambda *refs: plan_kernel(came, *refs),
        grid=(1,),
        out_shape=(
            jax.ShapeDtypeStruct((COLS, 8), jnp.int32),
            jax.ShapeDtypeStruct((1, NCTX * CAP), jnp.int32),
        ),
        in_specs=[pl.BlockSpec(memory_space=pltpu.SMEM), full(GROUP, COLS)],
        out_specs=(full(COLS, 8), full(1, NCTX * CAP)),
        compiler_params=pltpu.CompilerParams(vmem_limit_bytes=LIMIT),
        name="plan",
    )(place, vertical)


def band_kernel(halo, blocks, first_ref, q_ref, *refs):
    own = blocks - halo
    k_refs, v_refs = list(refs[:own]), list(refs[own : 2 * own])
    if halo:
        edge = refs[2 * own]
        k_refs = [edge.at[pl.ds(BAND - (halo - n) * PIECE, PIECE)] for n in range(halo)] + k_refs
        v_refs = [edge.at[pl.ds(2 * BAND - (halo - n) * PIECE, PIECE)] for n in range(halo)] + v_refs
    acc_ref, ml_ref, kx, vt = refs[-4:]
    step = pl.program_id(0)

    @pl.when(step == 0)
    def _():
        first = first_ref[0] != 0
        for n, (k_ref, v_ref) in enumerate(zip(k_refs, v_refs)):
            at = slice(n * PIECE, (n + 1) * PIECE)
            k, v, one = k_ref[...], v_ref[...], jnp.ones((VR - HEAD, PIECE), BF)
            if n < halo:
                k = jnp.where(first, jnp.broadcast_to(k_refs[halo][0:1, :], k.shape), k)
                v = jnp.where(first, jnp.zeros_like(v), v)
                one = jnp.where(first, jnp.zeros_like(one), one)
            kx[at, :] = k
            vt[:HEAD, at] = v.T
            vt[HEAD:, at] = one

    off = pl.multiple_of(step * QB, QB)
    tri = lax.broadcasted_iota(jnp.int32, (QB, QB), 0) <= lax.broadcasted_iota(jnp.int32, (QB, QB), 1)

    def heads(exact):
        scores = lambda h: dot_t(kx[pl.ds(off, BAND + QB), :], q_ref[:, h * HEAD : (h + 1) * HEAD])
        nxt = scores(0)
        for h in range(GROUP):
            s = nxt
            if h + 1 < GROUP:
                nxt = scores(h + 1)
            s_in = s[QB:BAND]
            s_edge = jnp.where(tri, s[BAND:], s[:QB])
            m = jnp.zeros((1, QB), F32)
            if exact:
                m = jnp.maximum(jnp.max(s_in, axis=0, keepdims=True), jnp.max(s_edge, axis=0, keepdims=True))
                s_in, s_edge = s_in - m, s_edge - m
            p_in = jnp.exp2(s_in * C).astype(BF)
            p_edge = jnp.exp2(s_edge * C)
            p_last = jnp.where(tri, p_edge, 0.0).astype(BF)
            p_first = jnp.where(tri, 0.0, p_edge).astype(BF)
            p = jnp.concatenate([p_first, p_in, p_last], 0)
            o = dot(vt[:, pl.ds(off, BAND + QB)], p)
            acc_ref[h * HEAD : (h + 1) * HEAD, :] = o[:HEAD]
            ml_ref[h : h + 1, :] = m
            ml_ref[GROUP + h : GROUP + h + 1, :] = o[HEAD : HEAD + 1]

    heads(False)
    total = ml_ref[GROUP:, :]
    unsafe = jnp.max(jnp.where((total > TINY) & (total < HUGE), 0.0, 1.0)) > 0.0

    @pl.when(unsafe)
    def _():
        heads(True)


def band(piece, span, first, queries, edge, keys, values, before):
    n = span * PIECE // QB
    blocks = span + BAND // PIECE
    halo = max(BAND // PIECE - piece, 0)
    start = piece * PIECE // QB
    kv, specs = [], []
    for array in (keys, values):
        for b in range(max(piece - BAND // PIECE, 0), piece + span):
            kv.append(array)
            specs.append(pl.BlockSpec((PIECE, HEAD), lambda i, b=b: (b, 0)))
    if halo:
        kv.append(edge)
        specs.append(pl.BlockSpec(memory_space=pltpu.VMEM))
    return pl.pallas_call(
        lambda *refs: band_kernel(halo, blocks, *refs),
        grid=(n,),
        out_shape=(
            jax.ShapeDtypeStruct((GROUP * HEAD, TOK), F32),
            jax.ShapeDtypeStruct((2 * GROUP, TOK), F32),
        ),
        in_specs=[
            pl.BlockSpec(memory_space=pltpu.SMEM),
            pl.BlockSpec((QB, GROUP * HEAD), lambda i: (start + i, 0)),
            *specs,
            *[pl.BlockSpec(memory_space=pl.ANY)] * len(before),
        ],
        out_specs=(
            pl.BlockSpec((GROUP * HEAD, QB), lambda i: (0, start + i)),
            pl.BlockSpec((2 * GROUP, QB), lambda i: (0, start + i)),
        ),
        scratch_shapes=[pltpu.VMEM((blocks * PIECE, HEAD), BF), pltpu.VMEM((VR, blocks * PIECE), BF)],
        input_output_aliases={2 + len(kv) + i: i for i in range(len(before))},
        compiler_params=pltpu.CompilerParams(vmem_limit_bytes=LIMIT),
        cost_estimate=pl.CostEstimate(
            flops=8 * span * PIECE * GROUP * HEAD * (BAND + QB),
            bytes_accessed=3 << 20,
            transcendentals=span * PIECE * BAND * GROUP,
        ),
        name="band",
    )(first, queries, *kv, *before)


def vert_kernel(nparts, *refs):
    base_ref, q_ref = refs[:2]
    g_refs = refs[2 : 2 + nparts]
    cols_ref, code_ref, a_ref, ml_ref, out_ref, kx, vt = refs[2 + nparts :]
    step = pl.program_id(0)

    @pl.when(step == 0)
    def _():
        for h in range(GROUP):
            mine = cols_ref[:, GROUP + h : GROUP + h + 1]
            t = None
            at = 0
            for g in g_refs:
                n = g.shape[0] * CAP
                sel = (mine == code_ref[:, at : at + n]).astype(F32).astype(BF)
                at += n
                part = dot(sel, g[:, h * CAP : (h + 1) * CAP, :].reshape(n, 2 * HEAD))
                t = part if t is None else t + part
            kx[h] = t[:, :HEAD].astype(BF)
            vt[h, :HEAD, :] = t[:, HEAD:].astype(BF).T
            vt[h, HEAD:, :] = jnp.ones((VR - HEAD, COLS), BF)

    qpos = base_ref[0] + step * QV - BAND + lax.broadcasted_iota(jnp.int32, (1, QV), 1)

    def heads(exact):
        scores = lambda h: dot_t(kx[h], q_ref[:, h * HEAD : (h + 1) * HEAD])
        nxt = scores(0)
        top = jnp.zeros((1, QV), F32)
        for h in range(GROUP):
            s = nxt
            if h + 1 < GROUP:
                nxt = scores(h + 1)
            s = jnp.where(cols_ref[:, h : h + 1] <= qpos, s, NEG)
            a = a_ref[h * HEAD : (h + 1) * HEAD, :]
            lb = ml_ref[GROUP + h : GROUP + h + 1, :]
            if exact:
                mb = ml_ref[h : h + 1, :]
                m = jnp.maximum(jnp.max(s, axis=0, keepdims=True), mb)
                s = s - m
                alpha = jnp.exp2((mb - m) * C)
                a, lb = a * alpha, lb * alpha
            p = jnp.exp2(s * C).astype(BF)
            o = dot(vt[h], p)
            top = jnp.maximum(top, jnp.where(o[HEAD : HEAD + 1] < HUGE, 0.0, 1.0))
            den = o[HEAD : HEAD + 1] + lb
            out_ref[:, h * HEAD : (h + 1) * HEAD] = ((a + o[:HEAD]) * (1.0 / den)).T.astype(BF)
        return top

    top = heads(False)
    unsafe = jnp.max(jnp.maximum(top, jnp.max(jnp.abs(ml_ref[:GROUP, :]), axis=0, keepdims=True))) > 0.0

    @pl.when(unsafe)
    def _():
        heads(True)


def vert(base, queries, parts, cols, code, acc, ml):
    n = TOK // QV
    full = lambda *s: pl.BlockSpec(s, lambda i: (0,) * len(s))
    return pl.pallas_call(
        lambda *refs: vert_kernel(len(parts), *refs),
        grid=(n,),
        out_shape=jax.ShapeDtypeStruct((TOK, GROUP * HEAD), BF),
        in_specs=[
            pl.BlockSpec(memory_space=pltpu.SMEM),
            pl.BlockSpec((QV, GROUP * HEAD), lambda i: (i, 0)),
            *[pl.BlockSpec(memory_space=pltpu.VMEM)] * len(parts),
            full(COLS, 8),
            full(1, NCTX * CAP),
            pl.BlockSpec((GROUP * HEAD, QV), lambda i: (0, i)),
            pl.BlockSpec((2 * GROUP, QV), lambda i: (0, i)),
        ],
        out_specs=pl.BlockSpec((QV, GROUP * HEAD), lambda i: (i, 0)),
        scratch_shapes=[pltpu.VMEM((GROUP, COLS, HEAD), BF), pltpu.VMEM((GROUP, VR, COLS), BF)],
        compiler_params=pltpu.CompilerParams(vmem_limit_bytes=VERT_LIMIT),
        cost_estimate=pl.CostEstimate(
            flops=8 * TOK * GROUP * HEAD * COLS,
            bytes_accessed=12 << 20,
            transcendentals=TOK * COLS * GROUP,
        ),
        name="vert",
    )(base, queries, *parts, cols, code, acc, ml)


AXES = ("ctx", "kvh")


def hop(array, grid, steps):
    ny, nz = grid
    nk = lax.axis_size("kvh")
    pairs = []
    for y in range(ny):
        for z in range(nz):
            for k in range(nk):
                dy, dz = steps[k % 2]
                to = ((y + dy) % ny) * nz + (z + dz) % nz
                pairs.append(((y * nz + z) * nk + k, to * nk + k))
    return lax.ppermute(array, AXES, pairs)


def shifted(came, steps):
    return [[(y - dy, z - dz) for y, z in c] for c, (dy, dz) in zip(came, steps)]


def joined(*lists):
    return [sum((c[core] for c in lists), []) for core in range(2)]


ROUND1 = (((0, 2), (0, -2)), ((0, 4), (0, -4)), ((0, -2), (0, 2)))
FAR = ((2, 0), (-2, 0))
NEAR = (((1, 0), (-1, 0)), ((0, 1), (0, -1)), ((1, 1), (-1, -1)))


def order():
    here = [[(0, 0)], [(0, 0)]]
    four = joined(here, *[shifted(here, s) for s in ROUND1])
    even = joined(four, shifted(four, FAR))
    return joined(even, *[shifted(even, s) for s in NEAR])


def shards(queries, keys, values, vertical):
    ctx = lax.axis_index("ctx")
    base = (ctx * TOK).astype(jnp.int32)[None]
    first = (ctx == 0).astype(jnp.int32)[None]
    grid = (4, 8)
    after = lambda x, *waits: lax.optimization_barrier((x, *waits))[0]

    own, edge = pick(base, vertical, keys, values)
    got = [hop(own, grid, s) for s in ROUND1]
    place = (ctx * 2 + lax.axis_index("kvh") % 2).astype(jnp.int32)[None]
    slots = plan(order(), place, after(vertical, own))

    four = jnp.concatenate([own] + got, 0)
    four, slots, queries = lax.optimization_barrier((four, slots, queries))
    far = hop(four, grid, FAR)
    state = band(3, 1, first, queries, None, keys, values, ())

    edge, far, *state = lax.optimization_barrier((edge, far, *state))
    edge = lax.ppermute(edge, "ctx", [(i, i + 1) for i in range(NCTX - 1)])
    state = band(2, 1, first, queries, None, keys, values, state)

    even = jnp.concatenate([four, far], 0)
    even, *state = lax.optimization_barrier((even, *state))
    near = [hop(even, grid, s) for s in NEAR]
    state = band(0, 2, first, queries, edge, keys, values, state)
    return vert(base, queries, [even, *near], *slots, *state)


def solution(mesh):
    in_specs = (P("ctx", "kvh"), P("ctx", "kvh"), P("ctx", "kvh"), P("kvh", None))
    return jax.shard_map(shards, mesh=mesh, in_specs=in_specs, out_specs=P("ctx", "kvh"), check_vma=False)
```

time: 71.6 us -> 85.9 us (1.20)
  the two profiles are of different devices: /device:TPU:8 before, /device:TPU:1 now
where the time goes in v3:
time: 85.9 us; the launch traced here: 84.6 us
  Pallas kernels  60.3 us (70%)
  starting transfers between devices  20.7 us (24%)
  local copies, waits for them, and re-layouts  1.96 us (2%)
  other arithmetic  0.92 us (1%)
    pallas_call x3, Pallas kernels, band(): pl.pallas_call(lambda *refs: band_kernel(halo, blocks, *refs), grid=(n,),...  36.7 us
    ppermute x7, starting transfers between devices, hop(): return lax.ppermute(array, AXES, pairs)  18.5 us
    pallas_call x1, Pallas kernels, vert(): pl.pallas_call(lambda *refs: vert_kernel(len(parts), *refs), grid=(n,), o...  17.9 us
    pallas_call x1, Pallas kernels, plan(): pl.pallas_call(lambda *refs: plan_kernel(came, *refs), grid=(1,), out_sha...  3.09 us
    pallas_call x1, Pallas kernels, pick(): pl.pallas_call(pick_kernel, grid=(1,), out_shape=(jax.ShapeDtypeStruct((1...  2.66 us
    ppermute x1, starting transfers between devices, shards(): edge = lax.ppermute(edge, 'ctx', [(i, i + 1) for i in range(NCTX - 1)])  2.22 us
    unnamed x12, local copies, waits for them, and re-layouts  1.96 us
  transfers between devices with their start and end apart: 8, of which 1 were waited for; matrix products, arithmetic and copies ran while one was open for 0% of the time, Pallas kernels for 47%

profile of v3, /device:TPU:1, one launch (start us, length us, event | category | flops | bytes accessed | tf_op | source)
XLA Modules:
  0.0 84.6 jit_solution(1495896662080647678)
XLA Ops:
  0.0 2.7 %pick.1 = (bf16[1,128,256]{2,1,0:T(8,128)(2,1)}, bf16[2048,128]{1,0:T(8,128)(2,1)}) custom-call(s32[1]{0:T(128)} %bitcast.base_ref.refs_0_, s32[4,512]{1,0:T(4,128)} %refs_1_, bf16[2048,128]{1,0:T(8,128)(2,1)} %refs_3_.5, bf16[2048,128]{1,0:T(8,128)(2,1)} %refs_5_.5), custom_call_target="tpu_custom_call" | custom-call | tf_op jit(solution)/shard_map/pick/pallas_call | solution.py:61
  2.7 3.8 %collective-permute-start.2 = (bf16[1,128,256]{2,1,0:T(8,128)(2,1)}, bf16[1,128,256]{2,1,0:T(8,128)(2,1)S(1)}, u32[]{:S(2)}, u32[]{:S(2)}) collective-permute-start(bf16[1,128,256]{2,1,0:T(8,128)(2,1)} %get-tuple-element.27), channel_id=1, source_target_pairs={{0,48},{1,17},{2,50},{3,19},{4,52},{5,21},{6,54},{7,23},{8,56},{9,... | collective-permute-start | bytes 196616 | tf_op jit(solution)/shard_map/ppermute | solution.py:316
  6.5 5.1 %collective-permute-start.1 = (bf16[1,128,256]{2,1,0:T(8,128)(2,1)}, bf16[1,128,256]{2,1,0:T(8,128)(2,1)S(1)}, u32[]{:S(2)}, u32[]{:S(2)}) collective-permute-start(bf16[1,128,256]{2,1,0:T(8,128)(2,1)} %get-tuple-element.27), channel_id=1, source_target_pairs={{0,32},{1,33},{2,34},{3,35},{4,36},{5,37},{6,38},{7,39},{8,40},{9,... | collective-permute-start | bytes 196616 | tf_op jit(solution)/shard_map/ppermute | solution.py:316
  11.6 2.4 %collective-permute-start = (bf16[1,128,256]{2,1,0:T(8,128)(2,1)}, bf16[1,128,256]{2,1,0:T(8,128)(2,1)S(1)}, u32[]{:S(2)}, u32[]{:S(2)}) collective-permute-start(bf16[1,128,256]{2,1,0:T(8,128)(2,1)} %get-tuple-element.27), channel_id=1, source_target_pairs={{0,16},{1,49},{2,18},{3,51},{4,20},{5,53},{6,22},{7,55},{8,24},{9,... | collective-permute-start | bytes 196616 | tf_op jit(solution)/shard_map/ppermute | solution.py:316
  14.0 3.1 %plan.1 = (s32[512,8]{1,0:T(8,128)}, s32[1,1024]{1,0:T(1,128)}) custom-call(s32[1]{0:T(128)} %bitcast.1.refs_0_, s32[4,512]{1,0:T(4,128)} %refs_1_), custom_call_target="tpu_custom_call" | custom-call | tf_op jit(solution)/shard_map/plan/pallas_call | solution.py:104
  17.1 0.0 collective-permute-done.2
  17.1 0.0 collective-permute-done.1
  17.1 0.5 collective-permute-done
  17.6 0.9 %pad_maximum_fusion.1 = bf16[4,128,256]{2,1,0:T(8,128)(2,1)S(1)} fusion(bf16[1,128,256]{2,1,0:T(8,128)(2,1)S(1)} %collective-permute-done.2, bf16[1,128,256]{2,1,0:T(8,128)(2,1)S(1)} %collective-permute-done.1, bf16[1,128,256]{2,1,0:T(8,128)(2,1)S(1)} %collective-permute-done, bf16[1,128,256]{2,1,0:T(8,128)(2,1)} %get-tuple-element.27), kind=kLoop, calls=%fused_computation.1 | loop fusion | flops 393216 | bytes 524288 | tf_op jit(solution)/shard_map/concatenate | solution.py:351
  18.4 3.0 %collective-permute-start.3 = (bf16[4,128,256]{2,1,0:T(8,128)(2,1)S(1)}, bf16[4,128,256]{2,1,0:T(8,128)(2,1)S(1)}, u32[]{:S(2)}, u32[]{:S(2)}) collective-permute-start(bf16[4,128,256]{2,1,0:T(8,128)(2,1)S(1)} %pad_maximum_fusion.1), channel_id=1, source_target_pairs={{0,128},{1,129},{2,130},{3,131},{4,132},{5,133},{6,134},{7,135},{8... | collective-permute-start | bytes 786440 | tf_op jit(solution)/shard_map/ppermute | solution.py:316
  21.4 0.0 copy-start.1
  21.4 9.7 %band.3 = (f32[512,2048]{1,0:T(8,128)}, f32[8,2048]{1,0:T(8,128)}) custom-call(s32[1]{0:T(128)} %bitcast.2.refs_0_, bf16[2048,512]{1,0:T(8,128)(2,1)} %refs_1_.4, bf16[2048,128]{1,0:T(8,128)(2,1)} %refs_3_.5, bf16[2048,128]{1,0:T(8,128)(2,1)} %refs_3_.5, bf16[2048,128]{1,0:T(8,128)(2,1)} %refs_3_.5, bf16[2048,128]{1,0:T(8,128)(2,1)} %refs_5_.5, ...), custom_call_target="tpu_custom_call" | custom-call | flops 2684354560 | bytes 3145728 | tf_op jit(solution)/shard_map/band/pallas_call | solution.py:190
  31.1 0.0 collective-permute-done.3
  31.1 0.0 copy-done.1
  31.1 2.2 %collective-permute-start.7 = (bf16[2048,128]{1,0:T(8,128)(2,1)S(1)}, bf16[2048,128]{1,0:T(8,128)(2,1)S(1)}, u32[]{:S(2)}, u32[]{:S(2)}) collective-permute-start(bf16[2048,128]{1,0:T(8,128)(2,1)S(1)} %copy-done.1), channel_id=1, source_target_pairs={{0,8},{8,16},{16,24},{24,32},{32,40},{40,48},{48,56},{56,64},{64,7... | collective-permute-start | bytes 1572872 | tf_op jit(solution)/shard_map/ppermute | solution.py:357
  33.4 0.0 copy-start
  33.4 9.9 %band.4 = (f32[512,2048]{1,0:T(8,128)}, f32[8,2048]{1,0:T(8,128)}) custom-call(s32[1]{0:T(128)} %bitcast.2.refs_0_, bf16[2048,512]{1,0:T(8,128)(2,1)} %refs_1_.4, bf16[2048,128]{1,0:T(8,128)(2,1)} %refs_3_.5, bf16[2048,128]{1,0:T(8,128)(2,1)} %refs_3_.5, bf16[2048,128]{1,0:T(8,128)(2,1)} %refs_3_.5, ...), custom_call_target="tpu_custom_call", output_to_operand_aliasing={{0}: (8, {}), {1}: (9, {})} | custom-call | flops 2684354560 | bytes 3145728 | tf_op jit(solution)/shard_map/band/pallas_call | solution.py:190
  43.3 2.1 %collective-permute-start.6 = (bf16[8,128,256]{2,1,0:T(8,128)(2,1)S(1)}, bf16[8,128,256]{2,1,0:T(8,128)(2,1)S(1)}, u32[]{:S(2)}, u32[]{:S(2)}) collective-permute-start(bf16[8,128,256]{2,1,0:T(8,128)(2,1)S(1)} %pad_maximum_fusion.refs_2_), channel_id=1, source_target_pairs={{0,72},{1,249},{2,74},{3,251},{4,76},{5,253},{6,78},{7,255},{8,80}... | collective-permute-start | bytes 1572872 | tf_op jit(solution)/shard_map/ppermute | solution.py:316
  45.4 2.1 %collective-permute-start.5 = (bf16[8,128,256]{2,1,0:T(8,128)(2,1)S(1)}, bf16[8,128,256]{2,1,0:T(8,128)(2,1)S(1)}, u32[]{:S(2)}, u32[]{:S(2)}) collective-permute-start(bf16[8,128,256]{2,1,0:T(8,128)(2,1)S(1)} %pad_maximum_fusion.refs_2_), channel_id=1, source_target_pairs={{0,8},{1,57},{2,10},{3,59},{4,12},{5,61},{6,14},{7,63},{8,16},{9,1... | collective-permute-start | bytes 1572872 | tf_op jit(solution)/shard_map/ppermute | solution.py:316
  47.5 0.0 copy-done
  47.5 0.0 collective-permute-start.4
  47.5 0.0 collective-permute-done.7.refs_6_
  47.5 0.0 copy-start.4
  47.5 0.8 copy-done.4
  48.3 17.1 %band.5 = (f32[512,2048]{1,0:T(8,128)}, f32[8,2048]{1,0:T(8,128)}) custom-call(s32[1]{0:T(128)} %bitcast.2.refs_0_, bf16[2048,512]{1,0:T(8,128)(2,1)} %refs_1_.4, bf16[2048,128]{1,0:T(8,128)(2,1)} %refs_3_.5, bf16[2048,128]{1,0:T(8,128)(2,1)} %refs_3_.5, bf16[2048,128]{1,0:T(8,128)(2,1)} %refs_5_.5, ...), custom_call_target="tpu_custom_call", output_to_operand_aliasing={{0}: (7, {}), {1}: (8, {})} | custom-call | flops 5368709120 | bytes 3145728 | tf_op jit(solution)/shard_map/band/pallas_call | solution.py:190
  65.4 0.0 collective-permute-done.6.refs_5_
  65.4 0.0 copy-start.2
  65.4 0.0 collective-permute-done.5.refs_4_
  65.4 0.0 copy-start.3
  65.5 0.0 collective-permute-done.4.refs_3_
  65.5 0.0 copy-start.5
  65.5 0.8 copy-done.2
  66.2 0.2 copy-done.3
  66.5 0.2 copy-done.5
  66.6 17.9 %vert.1 = bf16[2048,512]{1,0:T(8,128)(2,1)} custom-call(s32[1]{0:T(128)} %bitcast.base_ref.refs_0_, bf16[2048,512]{1,0:T(8,128)(2,1)} %refs_1_.4, bf16[8,128,256]{2,1,0:T(8,128)(2,1)} %copy-done, bf16[8,128,256]{2,1,0:T(8,128)(2,1)} %copy-done.5, bf16[8,128,256]{2,1,0:T(8,128)(2,1)} %copy-done.3, bf16[8,128,256]{2,1,0:T(8,128)(2,1)} %copy-done.2, ...), custom_call_target="tpu_custom_call" | custom-call | flops 4294967296 | bytes 12582912 | tf_op jit(solution)/shard_map/vert/pallas_call | solution.py:278
  (1 shorter events, 0.0 us)
Async XLA Ops:
  2.7 14.4 %collective-permute-start.2 = (bf16[1,128,256]{2,1,0:T(8,128)(2,1)}, bf16[1,128,256]{2,1,0:T(8,128)(2,1)S(1)}, u32[]{:S(2)}, u32[]{:S(2)}) collective-permute-start(bf16[1,128,256]{2,1,0:T(8,128)(2,1)} %get-tuple-element.27), channel_id=1, source_target_pairs={{0,48},{1,17},{2,50},{3,19},{4,52},{5,21},{6,54},{7,23},{8,56},{9,... | collective-permute-start | bytes 196616 | tf_op jit(solution)/shard_map/ppermute | solution.py:316
  6.5 10.6 %collective-permute-start.1 = (bf16[1,128,256]{2,1,0:T(8,128)(2,1)}, bf16[1,128,256]{2,1,0:T(8,128)(2,1)S(1)}, u32[]{:S(2)}, u32[]{:S(2)}) collective-permute-start(bf16[1,128,256]{2,1,0:T(8,128)(2,1)} %get-tuple-element.27), channel_id=1, source_target_pairs={{0,32},{1,33},{2,34},{3,35},{4,36},{5,37},{6,38},{7,39},{8,40},{9,... | collective-permute-start | bytes 196616 | tf_op jit(solution)/shard_map/ppermute | solution.py:316
  11.6 6.0 %collective-permute-start = (bf16[1,128,256]{2,1,0:T(8,128)(2,1)}, bf16[1,128,256]{2,1,0:T(8,128)(2,1)S(1)}, u32[]{:S(2)}, u32[]{:S(2)}) collective-permute-start(bf16[1,128,256]{2,1,0:T(8,128)(2,1)} %get-tuple-element.27), channel_id=1, source_target_pairs={{0,16},{1,49},{2,18},{3,51},{4,20},{5,53},{6,22},{7,55},{8,24},{9,... | collective-permute-start | bytes 196616 | tf_op jit(solution)/shard_map/ppermute | solution.py:316
  18.4 12.7 %collective-permute-start.3 = (bf16[4,128,256]{2,1,0:T(8,128)(2,1)S(1)}, bf16[4,128,256]{2,1,0:T(8,128)(2,1)S(1)}, u32[]{:S(2)}, u32[]{:S(2)}) collective-permute-start(bf16[4,128,256]{2,1,0:T(8,128)(2,1)S(1)} %pad_maximum_fusion.1), channel_id=1, source_target_pairs={{0,128},{1,129},{2,130},{3,131},{4,132},{5,133},{6,134},{7,135},{8... | collective-permute-start | bytes 786440 | tf_op jit(solution)/shard_map/ppermute | solution.py:316
  21.4 9.7 %copy-start.1 = (bf16[2048,128]{1,0:T(8,128)(2,1)S(1)}, bf16[2048,128]{1,0:T(8,128)(2,1)}, u32[]{:S(2)}) copy-start(bf16[2048,128]{1,0:T(8,128)(2,1)} %get-tuple-element.44) | copy-start | bytes 1572868
  31.1 16.4 %collective-permute-start.7 = (bf16[2048,128]{1,0:T(8,128)(2,1)S(1)}, bf16[2048,128]{1,0:T(8,128)(2,1)S(1)}, u32[]{:S(2)}, u32[]{:S(2)}) collective-permute-start(bf16[2048,128]{1,0:T(8,128)(2,1)S(1)} %copy-done.1), channel_id=1, source_target_pairs={{0,8},{8,16},{16,24},{24,32},{32,40},{40,48},{48,56},{56,64},{64,7... | collective-permute-start | bytes 1572872 | tf_op jit(solution)/shard_map/ppermute | solution.py:357
  33.4 14.1 %copy-start = (bf16[8,128,256]{2,1,0:T(8,128)(2,1)}, bf16[8,128,256]{2,1,0:T(8,128)(2,1)S(1)}, u32[]{:S(2)}) copy-start(bf16[8,128,256]{2,1,0:T(8,128)(2,1)S(1)} %pad_maximum_fusion.refs_2_) | copy-start | bytes 1572868
  43.3 22.2 %collective-permute-start.6 = (bf16[8,128,256]{2,1,0:T(8,128)(2,1)S(1)}, bf16[8,128,256]{2,1,0:T(8,128)(2,1)S(1)}, u32[]{:S(2)}, u32[]{:S(2)}) collective-permute-start(bf16[8,128,256]{2,1,0:T(8,128)(2,1)S(1)} %pad_maximum_fusion.refs_2_), channel_id=1, source_target_pairs={{0,72},{1,249},{2,74},{3,251},{4,76},{5,253},{6,78},{7,255},{8,80}... | collective-permute-start | bytes 1572872 | tf_op jit(solution)/shard_map/ppermute | solution.py:316
  45.4 20.1 %collective-permute-start.5 = (bf16[8,128,256]{2,1,0:T(8,128)(2,1)S(1)}, bf16[8,128,256]{2,1,0:T(8,128)(2,1)S(1)}, u32[]{:S(2)}, u32[]{:S(2)}) collective-permute-start(bf16[8,128,256]{2,1,0:T(8,128)(2,1)S(1)} %pad_maximum_fusion.refs_2_), channel_id=1, source_target_pairs={{0,8},{1,57},{2,10},{3,59},{4,12},{5,61},{6,14},{7,63},{8,16},{9,1... | collective-permute-start | bytes 1572872 | tf_op jit(solution)/shard_map/ppermute | solution.py:316
  47.5 18.0 %collective-permute-start.4 = (bf16[8,128,256]{2,1,0:T(8,128)(2,1)S(1)}, bf16[8,128,256]{2,1,0:T(8,128)(2,1)S(1)}, u32[]{:S(2)}, u32[]{:S(2)}) collective-permute-start(bf16[8,128,256]{2,1,0:T(8,128)(2,1)S(1)} %pad_maximum_fusion.refs_2_), channel_id=1, source_target_pairs={{0,64},{1,193},{2,66},{3,195},{4,68},{5,197},{6,70},{7,199},{8,72}... | collective-permute-start | bytes 1572872 | tf_op jit(solution)/shard_map/ppermute | solution.py:316
  47.5 0.8 copy-start.4
  65.4 0.8 copy-start.2
  65.4 1.0 %copy-start.3 = (bf16[8,128,256]{2,1,0:T(8,128)(2,1)}, bf16[8,128,256]{2,1,0:T(8,128)(2,1)S(1)}, u32[]{:S(2)}) copy-start(bf16[8,128,256]{2,1,0:T(8,128)(2,1)S(1)} %collective-permute-done.5.refs_4_) | copy-start | bytes 1572868
  65.5 1.2 %copy-start.5 = (bf16[8,128,256]{2,1,0:T(8,128)(2,1)}, bf16[8,128,256]{2,1,0:T(8,128)(2,1)S(1)}, u32[]{:S(2)}) copy-start(bf16[8,128,256]{2,1,0:T(8,128)(2,1)S(1)} %collective-permute-done.4.refs_3_) | copy-start | bytes 1572868

commit v4 on v3

--- a/solution.py
+++ b/solution.py
@@ -77,15 +77,14 @@
     y, z, core = place >> 4, (place >> 1) & 7, place & 1
     wide = jnp.concatenate([vert_ref[...].astype(F32), jnp.zeros((8 - GROUP, COLS), F32)], 0)
     cols = wide.T.astype(jnp.int32)
-    lanes = lax.broadcasted_iota(jnp.int32, (COLS, HEAD), 1)
     rows = lax.broadcasted_iota(jnp.int32, (COLS, 1), 0)
     lane8 = lax.broadcasted_iota(jnp.int32, (COLS, 8), 1)
+    one = jnp.ones((COLS, HEAD), BF)
     out = cols
     for h in range(GROUP):
-        v = cols[:, h : h + 1]
-        starts = jnp.sum((v < lanes * TOK).astype(jnp.int32), axis=0, keepdims=True)
-        d = v >> 11
-        start = jnp.sum(jnp.where(lanes == d, starts, 0), axis=1, keepdims=True)
+        d = cols[:, h : h + 1] >> 11
+        earlier = ((vert_ref[h : h + 1, :] >> 11) < d).astype(F32).astype(BF)
+        start = dot(earlier, one)[:, :8].astype(jnp.int32)
         out = jnp.where(lane8 == GROUP + h, d * CAP + rows - start, out)
     cols_ref[...] = out
     slot = lax.broadcasted_iota(jnp.int32, (1, NCTX * CAP), 1)
@@ -346,16 +345,14 @@
     own, edge = pick(base, vertical, keys, values)
     got = [hop(own, grid, s) for s in ROUND1]
     place = (ctx * 2 + lax.axis_index("kvh") % 2).astype(jnp.int32)[None]
-    slots = plan(order(), place, after(vertical, own))
 
     four = jnp.concatenate([own] + got, 0)
-    four, slots, queries = lax.optimization_barrier((four, slots, queries))
+    four, queries = lax.optimization_barrier((four, queries))
     far = hop(four, grid, FAR)
-    state = band(3, 1, first, queries, None, keys, values, ())
-
-    edge, far, *state = lax.optimization_barrier((edge, far, *state))
+    slots = plan(order(), place, after(vertical, four))
+    edge, slots = lax.optimization_barrier((edge, slots))
     edge = lax.ppermute(edge, "ctx", [(i, i + 1) for i in range(NCTX - 1)])
-    state = band(2, 1, first, queries, None, keys, values, state)
+    state = band(2, 2, first, after(queries, slots[0]), None, keys, values, ())
 
     even = jnp.concatenate([four, far], 0)
     even, *state = lax.optimization_barrier((even, *state))

time: 85.9 us -> 85.9 us (level)
  waiting for transfers between devices: 0.5 us -> 3.59 us
  Pallas kernels: 60.3 us -> 57.3 us
    ppermute x7, waiting for transfers between devices: 0.49 us -> 3.59 us  [hop(): return lax.ppermute(array, AXES, pairs)]
    pallas_call x3 -> x2, Pallas kernels: 36.7 us -> 34.3 us  [band(): pl.pallas_call(lambda *refs: band_kernel(halo, blocks, *refs), grid=(n,),...]
    unnamed x12 -> x10, local copies, waits for them, and re-layouts: 1.96 us -> 1.94 us
  transfers between devices with their start and end apart: 8 -> 8, of which waited for: 1 -> 2; matrix products, arithmetic and copies ran while one was open for 0% -> 0% of each run, Pallas kernels for 47% -> 43%
where the time goes in v4:
time: 85.9 us; the launch traced here: 84.6 us
  Pallas kernels  57.3 us (67%)
  starting transfers between devices  20.8 us (24%)
  waiting for transfers between devices  3.59 us (4%)
  local copies, waits for them, and re-layouts  1.94 us (2%)
  other arithmetic  0.92 us (1%)
    pallas_call x2, Pallas kernels, band(): pl.pallas_call(lambda *refs: band_kernel(halo, blocks, *refs), grid=(n,),...  34.3 us
    ppermute x7, starting transfers between devices, hop(): return lax.ppermute(array, AXES, pairs)  19.1 us
    pallas_call x1, Pallas kernels, vert(): pl.pallas_call(lambda *refs: vert_kernel(len(parts), *refs), grid=(n,), o...  17.9 us
    ppermute x7, waiting for transfers between devices, hop(): return lax.ppermute(array, AXES, pairs)  3.59 us
    pallas_call x1, Pallas kernels, pick(): pl.pallas_call(pick_kernel, grid=(1,), out_shape=(jax.ShapeDtypeStruct((1...  2.65 us
    pallas_call x1, Pallas kernels, plan(): pl.pallas_call(lambda *refs: plan_kernel(came, *refs), grid=(1,), out_sha...  2.4 us
    unnamed x10, local copies, waits for them, and re-layouts  1.94 us
  transfers between devices with their start and end apart: 8, of which 2 were waited for; matrix products, arithmetic and copies ran while one was open for 0% of the time, Pallas kernels for 43%

profile of v4, /device:TPU:1, one launch (start us, length us, event | category | flops | bytes accessed | tf_op | source)
XLA Modules:
  0.0 84.6 jit_solution(18351432845134136487)
XLA Ops:
  0.0 2.6 %pick.1 = (bf16[1,128,256]{2,1,0:T(8,128)(2,1)}, bf16[2048,128]{1,0:T(8,128)(2,1)}) custom-call(s32[1]{0:T(128)} %bitcast.base_ref.refs_0_, s32[4,512]{1,0:T(4,128)} %refs_1_, bf16[2048,128]{1,0:T(8,128)(2,1)} %refs_3_.3, bf16[2048,128]{1,0:T(8,128)(2,1)} %refs_5_.3), custom_call_target="tpu_custom_call" | custom-call | tf_op jit(solution)/shard_map/pick/pallas_call | solution.py:61
  2.6 3.8 %collective-permute-start.2 = (bf16[1,128,256]{2,1,0:T(8,128)(2,1)}, bf16[1,128,256]{2,1,0:T(8,128)(2,1)S(1)}, u32[]{:S(2)}, u32[]{:S(2)}) collective-permute-start(bf16[1,128,256]{2,1,0:T(8,128)(2,1)} %get-tuple-element.23), channel_id=1, source_target_pairs={{0,48},{1,17},{2,50},{3,19},{4,52},{5,21},{6,54},{7,23},{8,56},{9,... | collective-permute-start | bytes 196616 | tf_op jit(solution)/shard_map/ppermute | solution.py:315
  6.5 5.1 %collective-permute-start.1 = (bf16[1,128,256]{2,1,0:T(8,128)(2,1)}, bf16[1,128,256]{2,1,0:T(8,128)(2,1)S(1)}, u32[]{:S(2)}, u32[]{:S(2)}) collective-permute-start(bf16[1,128,256]{2,1,0:T(8,128)(2,1)} %get-tuple-element.23), channel_id=1, source_target_pairs={{0,32},{1,33},{2,34},{3,35},{4,36},{5,37},{6,38},{7,39},{8,40},{9,... | collective-permute-start | bytes 196616 | tf_op jit(solution)/shard_map/ppermute | solution.py:315
  11.6 2.4 %collective-permute-start = (bf16[1,128,256]{2,1,0:T(8,128)(2,1)}, bf16[1,128,256]{2,1,0:T(8,128)(2,1)S(1)}, u32[]{:S(2)}, u32[]{:S(2)}) collective-permute-start(bf16[1,128,256]{2,1,0:T(8,128)(2,1)} %get-tuple-element.23), channel_id=1, source_target_pairs={{0,16},{1,49},{2,18},{3,51},{4,20},{5,53},{6,22},{7,55},{8,24},{9,... | collective-permute-start | bytes 196616 | tf_op jit(solution)/shard_map/ppermute | solution.py:315
  14.0 0.0 collective-permute-done.2
  14.0 0.4 collective-permute-done.1
  14.4 3.2 %collective-permute-done = bf16[1,128,256]{2,1,0:T(8,128)(2,1)S(1)} collective-permute-done((bf16[1,128,256]{2,1,0:T(8,128)(2,1)}, bf16[1,128,256]{2,1,0:T(8,128)(2,1)S(1)}, u32[]{:S(2)}, u32[]{:S(2)}) %collective-permute-start) | collective-permute-done | bytes 65568 | tf_op jit(solution)/shard_map/ppermute | solution.py:315
  17.5 0.9 %pad_maximum_fusion.1 = bf16[4,128,256]{2,1,0:T(8,128)(2,1)S(1)} fusion(bf16[1,128,256]{2,1,0:T(8,128)(2,1)S(1)} %collective-permute-done.2, bf16[1,128,256]{2,1,0:T(8,128)(2,1)S(1)} %collective-permute-done.1, bf16[1,128,256]{2,1,0:T(8,128)(2,1)S(1)} %collective-permute-done, bf16[1,128,256]{2,1,0:T(8,128)(2,1)} %get-tuple-element.23), kind=kLoop, calls=%fused_computation.1 | loop fusion | flops 393216 | bytes 524288 | tf_op jit(solution)/shard_map/concatenate | solution.py:349
  18.4 3.0 %collective-permute-start.3 = (bf16[4,128,256]{2,1,0:T(8,128)(2,1)S(1)}, bf16[4,128,256]{2,1,0:T(8,128)(2,1)S(1)}, u32[]{:S(2)}, u32[]{:S(2)}) collective-permute-start(bf16[4,128,256]{2,1,0:T(8,128)(2,1)S(1)} %pad_maximum_fusion.1), channel_id=1, source_target_pairs={{0,128},{1,129},{2,130},{3,131},{4,132},{5,133},{6,134},{7,135},{8... | collective-permute-start | bytes 786440 | tf_op jit(solution)/shard_map/ppermute | solution.py:315
  21.4 2.4 %plan.1 = (s32[512,8]{1,0:T(8,128)}, s32[1,1024]{1,0:T(1,128)}) custom-call(s32[1]{0:T(128)} %bitcast.2.refs_0_, s32[4,512]{1,0:T(4,128)} %refs_1_), custom_call_target="tpu_custom_call" | custom-call | tf_op jit(solution)/shard_map/plan/pallas_call | solution.py:103
  23.8 1.6 %collective-permute-start.7 = (bf16[2048,128]{1,0:T(8,128)(2,1)}, bf16[2048,128]{1,0:T(8,128)(2,1)S(1)}, u32[]{:S(2)}, u32[]{:S(2)}) collective-permute-start(bf16[2048,128]{1,0:T(8,128)(2,1)} %get-tuple-element.36), channel_id=1, source_target_pairs={{0,8},{8,16},{16,24},{24,32},{32,40},{40,48},{48,56},{56,64},{64,7... | collective-permute-start | bytes 1572872 | tf_op jit(solution)/shard_map/ppermute | solution.py:354
  25.5 17.2 %band.2 = (f32[512,2048]{1,0:T(8,128)}, f32[8,2048]{1,0:T(8,128)}) custom-call(s32[1]{0:T(128)} %bitcast.1.refs_0_, bf16[2048,512]{1,0:T(8,128)(2,1)} %refs_1_.3, bf16[2048,128]{1,0:T(8,128)(2,1)} %refs_3_.3, bf16[2048,128]{1,0:T(8,128)(2,1)} %refs_3_.3, bf16[2048,128]{1,0:T(8,128)(2,1)} %refs_3_.3, bf16[2048,128]{1,0:T(8,128)(2,1)} %refs_3_.3, ...), custom_call_target="tpu_custom_call" | custom-call | flops 5368709120 | bytes 3145728 | tf_op jit(solution)/shard_map/band/pallas_call | solution.py:189
  42.7 0.0 collective-permute-done.3
  42.7 0.0 copy-start
  42.7 2.7 %collective-permute-start.6 = (bf16[8,128,256]{2,1,0:T(8,128)(2,1)S(1)}, bf16[8,128,256]{2,1,0:T(8,128)(2,1)S(1)}, u32[]{:S(2)}, u32[]{:S(2)}) collective-permute-start(bf16[8,128,256]{2,1,0:T(8,128)(2,1)S(1)} %pad_maximum_fusion.refs_2_), channel_id=1, source_target_pairs={{0,72},{1,249},{2,74},{3,251},{4,76},{5,253},{6,78},{7,255},{8,80}... | collective-permute-start | bytes 1572872 | tf_op jit(solution)/shard_map/ppermute | solution.py:315
  45.5 2.1 %collective-permute-start.5 = (bf16[8,128,256]{2,1,0:T(8,128)(2,1)S(1)}, bf16[8,128,256]{2,1,0:T(8,128)(2,1)S(1)}, u32[]{:S(2)}, u32[]{:S(2)}) collective-permute-start(bf16[8,128,256]{2,1,0:T(8,128)(2,1)S(1)} %pad_maximum_fusion.refs_2_), channel_id=1, source_target_pairs={{0,8},{1,57},{2,10},{3,59},{4,12},{5,61},{6,14},{7,63},{8,16},{9,1... | collective-permute-start | bytes 1572872 | tf_op jit(solution)/shard_map/ppermute | solution.py:315
  47.6 0.0 collective-permute-start.4
  47.6 0.0 collective-permute-done.7.refs_6_
  47.6 0.0 copy-start.3
  47.6 0.8 copy-done.3
  48.4 17.1 %band.3 = (f32[512,2048]{1,0:T(8,128)}, f32[8,2048]{1,0:T(8,128)}) custom-call(s32[1]{0:T(128)} %bitcast.1.refs_0_, bf16[2048,512]{1,0:T(8,128)(2,1)} %refs_1_.3, bf16[2048,128]{1,0:T(8,128)(2,1)} %refs_3_.3, bf16[2048,128]{1,0:T(8,128)(2,1)} %refs_3_.3, bf16[2048,128]{1,0:T(8,128)(2,1)} %refs_5_.3, ...), custom_call_target="tpu_custom_call", output_to_operand_aliasing={{0}: (7, {}), {1}: (8, {})} | custom-call | flops 5368709120 | bytes 3145728 | tf_op jit(solution)/shard_map/band/pallas_call | solution.py:189
  65.5 0.0 copy-done
  65.5 0.0 collective-permute-done.6.refs_5_
  65.5 0.0 copy-start.1
  65.5 0.0 collective-permute-done.5.refs_4_
  65.5 0.0 copy-start.2
  65.5 0.0 collective-permute-done.4.refs_3_
  65.5 0.0 copy-start.4
  65.5 0.8 copy-done.1
  66.3 0.2 copy-done.2
  66.5 0.2 copy-done.4
  66.7 17.9 %vert.1 = bf16[2048,512]{1,0:T(8,128)(2,1)} custom-call(s32[1]{0:T(128)} %bitcast.base_ref.refs_0_, bf16[2048,512]{1,0:T(8,128)(2,1)} %refs_1_.3, bf16[8,128,256]{2,1,0:T(8,128)(2,1)} %copy-done, bf16[8,128,256]{2,1,0:T(8,128)(2,1)} %copy-done.4, bf16[8,128,256]{2,1,0:T(8,128)(2,1)} %copy-done.2, bf16[8,128,256]{2,1,0:T(8,128)(2,1)} %copy-done.1, ...), custom_call_target="tpu_custom_call" | custom-call | flops 4294967296 | bytes 12582912 | tf_op jit(solution)/shard_map/vert/pallas_call | solution.py:277
  (1 shorter events, 0.0 us)
Async XLA Ops:
  2.6 11.3 %collective-permute-start.2 = (bf16[1,128,256]{2,1,0:T(8,128)(2,1)}, bf16[1,128,256]{2,1,0:T(8,128)(2,1)S(1)}, u32[]{:S(2)}, u32[]{:S(2)}) collective-permute-start(bf16[1,128,256]{2,1,0:T(8,128)(2,1)} %get-tuple-element.23), channel_id=1, source_target_pairs={{0,48},{1,17},{2,50},{3,19},{4,52},{5,21},{6,54},{7,23},{8,56},{9,... | collective-permute-start | bytes 196616 | tf_op jit(solution)/shard_map/ppermute | solution.py:315
  6.5 7.9 %collective-permute-start.1 = (bf16[1,128,256]{2,1,0:T(8,128)(2,1)}, bf16[1,128,256]{2,1,0:T(8,128)(2,1)S(1)}, u32[]{:S(2)}, u32[]{:S(2)}) collective-permute-start(bf16[1,128,256]{2,1,0:T(8,128)(2,1)} %get-tuple-element.23), channel_id=1, source_target_pairs={{0,32},{1,33},{2,34},{3,35},{4,36},{5,37},{6,38},{7,39},{8,40},{9,... | collective-permute-start | bytes 196616 | tf_op jit(solution)/shard_map/ppermute | solution.py:315
  11.6 6.0 %collective-permute-start = (bf16[1,128,256]{2,1,0:T(8,128)(2,1)}, bf16[1,128,256]{2,1,0:T(8,128)(2,1)S(1)}, u32[]{:S(2)}, u32[]{:S(2)}) collective-permute-start(bf16[1,128,256]{2,1,0:T(8,128)(2,1)} %get-tuple-element.23), channel_id=1, source_target_pairs={{0,16},{1,49},{2,18},{3,51},{4,20},{5,53},{6,22},{7,55},{8,24},{9,... | collective-permute-start | bytes 196616 | tf_op jit(solution)/shard_map/ppermute | solution.py:315
  18.4 24.2 %collective-permute-start.3 = (bf16[4,128,256]{2,1,0:T(8,128)(2,1)S(1)}, bf16[4,128,256]{2,1,0:T(8,128)(2,1)S(1)}, u32[]{:S(2)}, u32[]{:S(2)}) collective-permute-start(bf16[4,128,256]{2,1,0:T(8,128)(2,1)S(1)} %pad_maximum_fusion.1), channel_id=1, source_target_pairs={{0,128},{1,129},{2,130},{3,131},{4,132},{5,133},{6,134},{7,135},{8... | collective-permute-start | bytes 786440 | tf_op jit(solution)/shard_map/ppermute | solution.py:315
  23.8 23.7 %collective-permute-start.7 = (bf16[2048,128]{1,0:T(8,128)(2,1)}, bf16[2048,128]{1,0:T(8,128)(2,1)S(1)}, u32[]{:S(2)}, u32[]{:S(2)}) collective-permute-start(bf16[2048,128]{1,0:T(8,128)(2,1)} %get-tuple-element.36), channel_id=1, source_target_pairs={{0,8},{8,16},{16,24},{24,32},{32,40},{40,48},{48,56},{56,64},{64,7... | collective-permute-start | bytes 1572872 | tf_op jit(solution)/shard_map/ppermute | solution.py:354
  42.7 22.8 %copy-start = (bf16[8,128,256]{2,1,0:T(8,128)(2,1)}, bf16[8,128,256]{2,1,0:T(8,128)(2,1)S(1)}, u32[]{:S(2)}) copy-start(bf16[8,128,256]{2,1,0:T(8,128)(2,1)S(1)} %pad_maximum_fusion.refs_2_) | copy-start | bytes 1572868
  42.7 22.7 %collective-permute-start.6 = (bf16[8,128,256]{2,1,0:T(8,128)(2,1)S(1)}, bf16[8,128,256]{2,1,0:T(8,128)(2,1)S(1)}, u32[]{:S(2)}, u32[]{:S(2)}) collective-permute-start(bf16[8,128,256]{2,1,0:T(8,128)(2,1)S(1)} %pad_maximum_fusion.refs_2_), channel_id=1, source_target_pairs={{0,72},{1,249},{2,74},{3,251},{4,76},{5,253},{6,78},{7,255},{8,80}... | collective-permute-start | bytes 1572872 | tf_op jit(solution)/shard_map/ppermute | solution.py:315
  45.5 20.0 %collective-permute-start.5 = (bf16[8,128,256]{2,1,0:T(8,128)(2,1)S(1)}, bf16[8,128,256]{2,1,0:T(8,128)(2,1)S(1)}, u32[]{:S(2)}, u32[]{:S(2)}) collective-permute-start(bf16[8,128,256]{2,1,0:T(8,128)(2,1)S(1)} %pad_maximum_fusion.refs_2_), channel_id=1, source_target_pairs={{0,8},{1,57},{2,10},{3,59},{4,12},{5,61},{6,14},{7,63},{8,16},{9,1... | collective-permute-start | bytes 1572872 | tf_op jit(solution)/shard_map/ppermute | solution.py:315
  47.6 18.0 %collective-permute-start.4 = (bf16[8,128,256]{2,1,0:T(8,128)(2,1)S(1)}, bf16[8,128,256]{2,1,0:T(8,128)(2,1)S(1)}, u32[]{:S(2)}, u32[]{:S(2)}) collective-permute-start(bf16[8,128,256]{2,1,0:T(8,128)(2,1)S(1)} %pad_maximum_fusion.refs_2_), channel_id=1, source_target_pairs={{0,64},{1,193},{2,66},{3,195},{4,68},{5,197},{6,70},{7,199},{8,72}... | collective-permute-start | bytes 1572872 | tf_op jit(solution)/shard_map/ppermute | solution.py:315
  47.6 0.8 copy-start.3
  65.5 0.8 copy-start.1
  65.5 1.0 %copy-start.2 = (bf16[8,128,256]{2,1,0:T(8,128)(2,1)}, bf16[8,128,256]{2,1,0:T(8,128)(2,1)S(1)}, u32[]{:S(2)}) copy-start(bf16[8,128,256]{2,1,0:T(8,128)(2,1)S(1)} %collective-permute-done.5.refs_4_) | copy-start | bytes 1572868
  65.5 1.1 %copy-start.4 = (bf16[8,128,256]{2,1,0:T(8,128)(2,1)}, bf16[8,128,256]{2,1,0:T(8,128)(2,1)S(1)}, u32[]{:S(2)}) copy-start(bf16[8,128,256]{2,1,0:T(8,128)(2,1)S(1)} %collective-permute-done.4.refs_3_) | copy-start | bytes 1572868
